TPU v7x, 32 devices: a whole 2x2x4 slice. The times are simulated.
32 devices in a mesh: dp: 8 (over z, core), expert: 4 (over y, x).
Axes of the slice: x: 2, y: 2, z: 4, core: 2. Of those that a mesh axis runs over, the one named last changes fastest.
Arguments:
- tokens: bfloat16 [4096, 2560], P(('dp', 'expert')), may hold values from -6 to 6
- out_grad: bfloat16 [4096, 2560], P(('dp', 'expert')), may hold values from -0.29882812 to 0.29882812
- gate_up: bfloat16 [4096, 1, 1536], P(('dp', 'expert')), may hold values from -8 to 8
- route_weight: bfloat16 [4096, 1], P(('dp', 'expert')), may hold values from 0.19921875 to 1
- routes: int32 [4096, 1], P(('dp', 'expert')), may hold values from 0 to 3; in each aligned block of 128 rows (0 to 127, 128 to 255, ...) at most 64 rows name the same one
- down_weight: bfloat16 [4, 768, 2560], P('expert', 'dp'), may hold values from -0.21875 to 0.21875
- master: float32 [4, 8, 506880], P('expert', 'dp'), may hold values from -0.12 to 0.12
- moment_one: float32 [4, 8, 506880], P('expert', 'dp'), may hold values from -2 to 2
- moment_two: float32 [4, 8, 506880], P('expert', 'dp'), may hold values from 0.05 to 5
- offsets: int32 [9], replicated, may hold values from 0 to 3932160, as said below
Outputs:
- new_master: float32 [4, 8, 506880], P('expert', 'dp')
- new_moment_one: float32 [4, 8, 506880], P('expert', 'dp')
- new_moment_two: float32 [4, 8, 506880], P('expert', 'dp')
- new_weight: bfloat16 [4, 2560, 1536], P('expert', 'dp')
- router_grad: float32 [4096, 1], P(('dp', 'expert'))
Inputs may be any that keep to these rules, and one draw needn't show every extreme that they name: `routes`: in each aligned block of 128 tokens (the tokens of one device) no expert is named more than 64 times, a bound that some block reaches; the 1 choices of a token differ. offsets[0] = 0, offsets[8] = 3932160; for 0 < j < 8, offsets[j] lies from j * 491520 - 15360 to j * 491520 - 2; offsets[7] = 3425280, so the last bucket holds exactly 506880 entries.
All inputs are finite; a program needn't handle non-finite values.
Results may differ from a plain program's by a relative error of at most 0.0012.
Values may be sent and summed in bfloat16 or wider, within the bound.
No kernel may reach another device: no remote copies, remote signals or barrier semaphores. Data moves between devices by JAX's collectives and lax.ppermute only.
A program may use at most 128 MiB of HBM per device.

v0:
```python
import functools

import jax
import jax.numpy as jnp
from jax import lax
from jax.experimental import pallas as pl
from jax.experimental.pallas import tpu as pltpu
from jax.sharding import PartitionSpec as P

beta_one = 0.9
beta_two = 0.95
learn_rate = 0.001
decay_rate = 0.1
adam_eps = 1e-08
adam_step = 20.0

LANES = 128
CHUNK = 120

f32 = jnp.float32
bf16 = jnp.bfloat16
i32 = jnp.int32


def round_up(value, unit):
    return -(-value // unit) * unit


def iota(shape, axis):
    return lax.broadcasted_iota(i32, shape, axis)


def params(mib):
    return pltpu.CompilerParams(vmem_limit_bytes=mib * 1024 * 1024)


def cost(flops, moved):
    return pl.CostEstimate(flops=int(flops), bytes_accessed=int(moved), transcendentals=0)


def pack_kernel(
    routes_ref, weight_ref, grads_any, saved_any, select_ref, target_ref, packed_any, grads, saved, packed, sems
):
    loads = [
        pltpu.make_async_copy(grads_any, grads, sems.at[0]),
        pltpu.make_async_copy(saved_any, saved, sems.at[1]),
    ]
    for load in loads:
        load.start()
    ids = routes_ref[...]
    experts, cap, _ = packed.shape
    count = ids.shape[1]
    width = grads.shape[1]
    hits = iota((round_up(experts, 8), count), 0) == ids
    before = (iota((count, count), 0) < iota((count, count), 1)).astype(bf16)
    earlier = jnp.dot(hits.astype(f32).astype(bf16), before, preferred_element_type=f32)
    slot = jnp.sum(jnp.where(hits, earlier, 0.0), axis=0, keepdims=True)
    target = ids * cap + slot.astype(i32)
    chosen = iota((experts * cap, count), 0) == target
    select = chosen.astype(f32).astype(bf16)
    select_ref[...] = chosen.astype(f32)
    target_ref[...] = target.astype(f32)
    weight = jnp.sum(jnp.where(chosen, weight_ref[...].astype(f32), 0.0), axis=1, keepdims=True)
    weight = jnp.broadcast_to(weight, (experts * cap, LANES)).astype(bf16)
    for load in loads:
        load.wait()
    picked_grads = jnp.dot(select, grads[...], preferred_element_type=f32).astype(bf16)
    picked_saved = jnp.dot(select, saved[...], preferred_element_type=f32).astype(bf16)
    stores = []
    for k in range(experts):
        span = slice(k * cap, (k + 1) * cap)
        packed[k, :, :width] = picked_grads[span]
        packed[k, :, width:-LANES] = picked_saved[span]
        packed[k, :, -LANES:] = weight[span]
        stores.append(pltpu.make_async_copy(packed.at[k], packed_any.at[k], sems.at[2 + k]))
        stores[-1].start()
    for store in stores:
        store.wait()


def window_kernel(target_ref, tokens_ref, out_ref, *, per, lead):
    parts, count, width = out_ref.shape
    diagonal = iota((count, count), 0) == iota((count, count), 1)
    column = jnp.sum(jnp.where(diagonal, target_ref[...], 0.0), axis=1, keepdims=True)
    note = jnp.broadcast_to(column, (count, width)).astype(bf16)
    lane = iota((count, width), 1)
    for j in range(parts):
        start = per * j - lead
        if start < 0:
            blank = jnp.zeros((count, -start), bf16)
            piece = jnp.concatenate([blank, tokens_ref[:, : start + width]], axis=1)
        else:
            piece = tokens_ref[:, start : start + width]
        out_ref[j] = jnp.where(lane == 0, note, piece)


def compact_kernel(position_ref, windows_ref, scores_ref, out_ref):
    parts, count, width = windows_ref.shape
    experts, _, cap, _ = out_ref.shape
    diagonal = iota((count, count), 0) == iota((count, count), 1)
    slots = iota((experts * cap, count), 0)
    for i in range(parts):
        block = windows_ref[i]
        column = block[:, 0:1].astype(f32)
        target = jnp.sum(jnp.where(diagonal, column, 0.0), axis=0, keepdims=True).astype(i32)
        select = (slots == target).astype(f32).astype(bf16)
        rows = jnp.dot(select, block, preferred_element_type=f32).astype(bf16)
        for k in range(experts):
            out_ref[k, i] = rows[k * cap : (k + 1) * cap]
    lane = iota((cap, LANES), 1)
    for k in range(experts):
        rest = scores_ref[k * cap : (k + 1) * cap, :]
        first = out_ref[k, position_ref[0], :, :LANES]
        for c in range(3):
            part = rest.astype(bf16)
            rest = rest - part.astype(f32)
            first = jnp.where(lane == 1 + c, part, first)
        out_ref[k, position_ref[0], :, :LANES] = first


def turn_kernel(rows_ref, out_ref):
    experts, parts, _, width = rows_ref.shape
    kept = out_ref.shape[1]
    for i in range(parts):
        slab = jnp.concatenate([rows_ref[k, i] for k in range(experts)], axis=0)
        out_ref[i] = slab.T[width - kept :, :]


def factor_kernel(arrived_ref, grads_ref, gate_ref, up_ref, score_ref):
    width, hidden = grads_ref.shape[1], gate_ref.shape[1]
    grads_ref[...] = arrived_ref[:, :width]
    gate = arrived_ref[:, width : width + hidden].astype(f32)
    up = arrived_ref[:, width + hidden : width + 2 * hidden].astype(f32)
    weight = arrived_ref[:, width + 2 * hidden :].astype(f32)[:, 0:1]
    sig = jax.nn.sigmoid(gate)
    act = gate * sig
    score_ref[...] = act * up
    up_ref[...] = weight * act
    gate_ref[...] = weight * (up * sig * (1.0 + gate * (1.0 - sig)))


def row_kernel(position_ref, grads_ref, gate_factor, up_factor, score_factor, *refs, chips):
    down_refs, refs = refs[:-6], refs[-5:]
    joined_any, scores_ref, joined, down, sems = refs
    hidden = down.shape[0]
    loads = []
    for n, down_ref in enumerate(down_refs):
        size = down_ref.shape[0]
        if size == hidden:
            at = 0
        else:
            slab = lax.rem(position_ref[0] + 2 * (chips - n // 2), 2 * chips) ^ (n % 2)
            at = pl.multiple_of(slab * size, 16)
        loads.append(pltpu.make_async_copy(down_ref, down.at[pl.ds(at, size)], sems.at[n]))
    for load in loads:
        load.start()
    for load in loads:
        load.wait()
    scores = None
    step = 2 * LANES
    stores = []
    for at in range(0, hidden, step):
        span = slice(at, at + step)
        back = lax.dot_general(
            grads_ref[...], down[span, :], (((1,), (1,)), ((), ())), preferred_element_type=f32
        )
        part = jnp.sum(score_factor[:, span] * back, axis=1, keepdims=True)
        scores = part if scores is None else scores + part
        for half, factor in enumerate((gate_factor, up_factor)):
            out = slice(half * hidden + at, half * hidden + at + step)
            joined[:, out] = (factor[:, span] * back).astype(bf16)
            sem = sems.at[len(down_refs) + 2 * (at // step) + half]
            stores.append(pltpu.make_async_copy(joined.at[:, out], joined_any.at[:, out], sem))
            stores[-1].start()
    scores_ref[...] = jnp.broadcast_to(scores, scores_ref.shape)
    for store in stores:
        store.wait()


def router_kernel(position_ref, select_ref, rows_ref, out_ref):
    experts = rows_ref.shape[0]
    own = [rows_ref[k, position_ref[0], :, :LANES] for k in range(experts)]
    parts = jnp.concatenate(own, axis=0).astype(f32)
    scores = (parts[:, 1:2] + parts[:, 2:3]) + parts[:, 3:4]
    out_ref[...] = jnp.sum(jnp.where(select_ref[...] > 0.5, scores, 0.0), axis=0, keepdims=True)


def head_kernel(master_ref, first_ref, second_ref, out_ref):
    for n, source in enumerate((master_ref, first_ref, second_ref)):
        out_ref[n] = source[...]


def ready_kernel(*refs):
    refs[-1][...] = jnp.zeros(refs[-1].shape, f32)


def slab_sum(total, turned_ref, slabs, joined_refs, span):
    for slab, ref in zip(slabs, joined_refs):
        piece = jnp.dot(turned_ref[slab], ref[:, span], preferred_element_type=f32)
        piece = piece.astype(bf16).astype(f32)
        total = piece if total is None else total + piece
    return total


def slabs_of(position, steps, chips):
    own = [lax.rem(position + 2 * (chips - k), 2 * chips) for k in steps]
    return [slab ^ other for slab in own for other in (0, 1)]


def early_kernel(position_ref, turned_ref, *refs, steps, chips):
    joined_refs, base, sum_ref = refs[: 2 * len(steps)], refs[2 * len(steps) : -1], refs[-1]
    step = 2 * LANES
    slabs = slabs_of(position_ref[0], steps, chips)
    for at in range(0, sum_ref.shape[1], step):
        span = slice(at, at + step)
        total = base[0][:, span] if base else None
        sum_ref[:, span] = slab_sum(total, turned_ref, slabs, joined_refs, span)


def adam(grad, old, first, second):
    first_new = beta_one * first + (1.0 - beta_one) * grad
    second_new = beta_two * second + (1.0 - beta_two) * grad * grad
    below = jnp.sqrt(second_new * (1.0 / (1.0 - beta_two**adam_step))) + adam_eps
    update = first_new * (learn_rate / (1.0 - beta_one**adam_step)) / below
    return old * (1.0 - learn_rate * decay_rate) - update, first_new, second_new


def final_kernel(
    position_ref,
    offsets_ref,
    turned_ref,
    early_ref,
    heads_ref,
    own_ref,
    other_ref,
    old,
    first,
    second,
    out_master,
    out_first,
    out_second,
    weight_ref,
    sums,
    moved,
    new_old,
    new_first,
    new_second,
    head_new,
    sems,
    *,
    even_size,
    head_rows,
    chips,
):
    kept, columns = early_ref.shape
    per = weight_ref.shape[0]
    lines = columns // LANES
    before = (kept - per) * lines
    bucket_rows = old.shape[0]
    flat_rows = even_size // LANES
    position = position_ref[0]
    start = offsets_ref[position]
    finish = offsets_ref[position + 1]
    shift = position * even_size - start
    next_shift = (position + 1) * even_size - finish
    length = finish - start
    whole, part = shift // LANES, shift % LANES
    odd = whole % 8
    next_whole, next_part = next_shift // LANES, next_shift % LANES

    step = 2 * LANES
    slabs = slabs_of(position, [chips - 1], chips)
    for begin in range(0, columns, step):
        span = slice(begin, begin + step)
        total = slab_sum(early_ref[:, span], turned_ref, slabs, (own_ref, other_ref), span)
        for c in range(step // LANES):
            block = pltpu.roll(total[:, c * LANES : (c + 1) * LANES], part, 1)
            line = begin // LANES + c
            sums[pl.ds(odd + line, kept, stride=lines), :] = block
            moved[pl.ds(odd + line + 1, kept, stride=lines), :] = block

    def slots_of(row, count):
        at = pl.multiple_of(row + before - (whole - odd), 8)
        lane = iota((count, LANES), 1)
        return jnp.where(lane >= part, sums[pl.ds(at, count), :], moved[pl.ds(at, count), :])

    def update(row, count):
        span = pl.ds(row, count)
        a, b, c = adam(slots_of(row, count), old[span, :], first[span, :], second[span, :])
        new_old[span, :], new_first[span, :], new_second[span, :] = a, b, c

    def masked(row, count):
        span = pl.ds(row, count)
        inside = (row + iota((count, LANES), 0)) * LANES + iota((count, LANES), 1) < length
        grad = jnp.where(inside, slots_of(row, count), 0.0)
        a, b, c = adam(grad, old[span, :], first[span, :], second[span, :])
        new_old[span, :] = jnp.where(inside, a, 0.0)
        new_first[span, :] = jnp.where(inside, b, 0.0)
        new_second[span, :] = jnp.where(inside, c, 0.0)

    def send(begin, count, slot):
        span = pl.ds(begin, count)
        stores = [
            pltpu.make_async_copy(source.at[span], target.at[span], sems.at[slot, n])
            for n, (source, target) in enumerate(
                ((new_old, out_master), (new_first, out_first), (new_second, out_second))
            )
        ]
        for store in stores:
            store.start()
        return stores

    def chunk(n, carry):
        update(pl.multiple_of(n * CHUNK, 8), CHUNK)
        return carry

    safe = (flat_rows - head_rows) // CHUNK
    third = -(-safe // 3)
    stores = []
    for slot, begin in enumerate(range(0, safe, third)):
        end = min(begin + third, safe)
        lax.fori_loop(begin, end, chunk, 0)
        stores += send(begin * CHUNK, (end - begin) * CHUNK, slot)
    for row in range(safe * CHUNK, bucket_rows, CHUNK):
        masked(row, min(CHUNK, bucket_rows - row))
    stores += send(safe * CHUNK, bucket_rows - safe * CHUNK, 3)

    def next_slots():
        lane = iota((head_rows, LANES), 1)
        base = flat_rows + before - next_whole + odd
        here = pltpu.roll(sums[pl.ds(base, head_rows), :], (LANES - part) % LANES, 1)
        above = pltpu.roll(sums[pl.ds(base - 1, head_rows), :], (LANES - part) % LANES, 1)
        return pltpu.roll(jnp.where(lane < LANES - next_part, here, above), next_part, 1)

    edge = round_up(-(-head_rows // lines), 16)
    head_new[pl.ds(edge * lines, head_rows), :] = adam(next_slots(), heads_ref[0], heads_ref[1], heads_ref[2])[0]

    flat_row = iota((edge, LANES), 0) + (per - edge)
    for c in range(lines):
        lane = iota((per, LANES), 1)
        here = new_old[pl.ds(c + whole, per, stride=lines), :]
        below = new_old[pl.ds(c + whole + 1, per, stride=lines), :]
        own = pltpu.roll(jnp.where(lane >= part, here, below), (LANES - part) % LANES, 1)
        base = c + next_whole
        lane = iota((edge, LANES), 1)
        here = head_new[pl.ds(base, edge, stride=lines), :]
        below = head_new[pl.ds(base + 1, edge, stride=lines), :]
        other = pltpu.roll(jnp.where(lane >= next_part, here, below), (LANES - next_part) % LANES, 1)
        flat = (flat_row * lines + c) * LANES + lane
        last = jnp.where(flat < even_size - next_shift, own[per - edge :], other)
        out = slice(c * LANES, (c + 1) * LANES)
        if per > edge:
            weight_ref[: per - edge, out] = own[: per - edge].astype(bf16)
        weight_ref[per - edge :, out] = last.astype(bf16)

    for store in stores:
        store.wait()


def vmem():
    return pl.BlockSpec(memory_space=pltpu.VMEM)


def anywhere():
    return pl.BlockSpec(memory_space=pl.ANY)


def hbm():
    return pl.BlockSpec(memory_space=pltpu.HBM)


def smem():
    return pl.BlockSpec(memory_space=pltpu.SMEM)


def call(kernel, outs, scalars, args, name, mib, flops=0, moved=0):
    many = isinstance(outs, (list, tuple))
    return pl.pallas_call(
        kernel,
        out_shape=outs,
        in_specs=[smem()] * len(scalars) + [vmem()] * len(args),
        out_specs=[vmem()] * len(outs) if many else vmem(),
        compiler_params=params(mib),
        cost_estimate=cost(flops, moved),
        name=name,
    )(*scalars, *args)


def struct(shape, kind):
    return jax.ShapeDtypeStruct(shape, kind)


def shards(
    tokens,
    out_grad,
    gate_up,
    route_weight,
    routes,
    down_weight,
    master,
    moment_one,
    moment_two,
    offsets,
):
    token_count, model_width = tokens.shape
    columns = gate_up.shape[2]
    hidden = columns // 2
    bucket_cap = master.shape[2]
    groups = lax.axis_size("expert")
    parts = lax.axis_size("dp")
    experts = groups * master.shape[0]
    cap = 2 * token_count // experts
    rows = experts * cap
    per = model_width // parts
    even_size = per * columns
    margin = bucket_cap - even_size
    extra = round_up(-(-margin // columns), 16)
    width = round_up(per + extra + 4, LANES)
    kept = per + extra
    lines = columns // LANES
    bucket_rows = bucket_cap // LANES
    head_rows = round_up(margin // LANES, 8)

    chips = parts // 2
    position = lax.axis_index("dp").astype(i32).reshape(1)
    state = struct((bucket_rows, LANES), f32)
    old, first, second = (array.reshape(bucket_rows, LANES) for array in (master, moment_one, moment_two))

    def onward(block):
        return lax.ppermute(block, "dp", [(i, (i + 2) % parts) for i in range(parts)])

    def swapped(block):
        return lax.ppermute(block, "dp", [(i, i ^ 1) for i in range(parts)])

    def exchanged(block, axis):
        return lax.all_to_all(block, axis, split_axis=0, concat_axis=0, tiled=True)

    def tied(*values):
        return lax.optimization_barrier(values)

    wide = model_width + columns + LANES
    select, target, packed = pl.pallas_call(
        pack_kernel,
        out_shape=[
            struct((rows, token_count), f32),
            struct((1, token_count), f32),
            struct((experts, cap, wide), bf16),
        ],
        in_specs=[vmem(), vmem(), hbm(), hbm()],
        out_specs=[vmem(), vmem(), hbm()],
        scratch_shapes=[
            pltpu.VMEM((token_count, model_width), bf16),
            pltpu.VMEM((token_count, columns), bf16),
            pltpu.VMEM((experts, cap, wide), bf16),
            pltpu.SemaphoreType.DMA((2 + experts,)),
        ],
        compiler_params=params(16),
        cost_estimate=cost(0, 6_000_000),
        name="pack",
    )(
        routes.reshape(1, token_count),
        route_weight.reshape(1, token_count),
        out_grad,
        gate_up.reshape(token_count, columns),
    )
    windows = call(
        functools.partial(window_kernel, per=per, lead=width - per),
        struct((parts, token_count, width), bf16),
        (),
        (target, tokens),
        "window",
        12,
        moved=2_000_000,
    )
    if down_weight.shape[1] % 16 == 0:
        held, other = [down_weight[0]], [swapped(down_weight[0])]
        for k in range(1, chips):
            arrival = onward(held[-1])
            if k == 1:
                arrival, windows = tied(arrival, windows)
            else:
                arrival, other = tied(arrival, other)
            held.append(arrival)
            other.append(swapped(arrival))
            if k == chips - 1:
                windows, held[-1] = tied(windows, held[-1])
        down = [piece for pair in zip(held, other) for piece in pair]
    else:
        down = [lax.all_gather(down_weight, "dp", axis=1, tiled=True)[0]]
        windows, down[0] = tied(windows, down[0])
    arrived = exchanged(packed, "expert").reshape(rows, wide)
    windows = exchanged(windows, "dp")
    factors = call(
        factor_kernel,
        [struct((rows, model_width), bf16)] + [struct((rows, hidden), f32)] * 3,
        (),
        (arrived,),
        "factors",
        20,
        moved=6_000_000,
    )
    ready = pl.pallas_call(
        ready_kernel,
        out_shape=struct((8, LANES), f32),
        in_specs=[anywhere()],
        out_specs=vmem(),
        compiler_params=params(4),
        cost_estimate=cost(0, 18_000_000),
        name="ready",
    )(down[-1])
    joined, scores = pl.pallas_call(
        functools.partial(row_kernel, chips=chips),
        out_shape=[struct((rows, columns), bf16), struct((rows, LANES), f32)],
        in_specs=[smem()] + [vmem()] * 4 + [anywhere()] * (len(down) + 1),
        out_specs=[hbm(), vmem()],
        scratch_shapes=[
            pltpu.VMEM((rows, columns), bf16),
            pltpu.VMEM((hidden, model_width), bf16),
            pltpu.SemaphoreType.DMA((len(down) + 2 * (hidden // (2 * LANES)),)),
        ],
        compiler_params=params(24),
        cost_estimate=cost(2 * rows * model_width * hidden, 8_000_000),
        name="rows",
    )(position, *factors, *down, ready)

    steps = [[joined, swapped(joined)]]
    step_one = onward(joined)
    heads = pl.pallas_call(
        head_kernel,
        grid=(1,),
        out_shape=struct((3, head_rows, LANES), f32),
        in_specs=[pl.BlockSpec((head_rows, LANES), lambda i: (0, 0))] * 3,
        out_specs=pl.BlockSpec((3, head_rows, LANES), lambda i: (0, 0, 0)),
        cost_estimate=cost(0, 400_000),
        name="heads",
    )(old, first, second)
    heads, _ = tied(heads, step_one)
    heads = lax.ppermute(heads, "dp", [(i + 1, i) for i in range(parts - 1)])
    compacted = call(
        compact_kernel,
        struct((experts, parts, cap, width), bf16),
        (position,),
        (windows, scores),
        "compact",
        12,
        moved=3_000_000,
    )
    compacted_rows = exchanged(compacted, "expert")
    turned = call(
        turn_kernel,
        struct((parts, kept, rows), bf16),
        (),
        (compacted_rows,),
        "turn",
        12,
        moved=3_000_000,
    )
    router_grad = call(
        router_kernel,
        struct((1, token_count), f32),
        (position,),
        (select, compacted_rows),
        "router",
        4,
        moved=300_000,
    )

    def early(name, at, pieces, sum_before):
        return call(
            functools.partial(early_kernel, steps=at, chips=chips),
            struct((kept, columns), f32),
            (position,),
            [turned] + pieces + sum_before,
            name,
            24,
            flops=4 * len(at) * rows * kept * columns,
            moved=8_000_000,
        )

    total = []
    arrival = joined
    for k in range(1, chips):
        arrival = onward(arrival) if k > 1 else step_one
        if k > 2:
            pieces = steps.pop()
            if k == 3:
                begun = early("early1", [0, 1], steps.pop(0) + steps.pop(0), [])
                total = [begun]
            total = [early("early%d" % (k - 1), [k - 1], pieces, total)]
        if k == chips - 1:
            arrival, total[0], router_grad, heads = tied(arrival, total[0], router_grad, heads)
        steps.append([arrival, swapped(arrival)])
    last = steps.pop()
    flat_rows = even_size // LANES
    sum_rows = round_up(kept * lines + head_rows + 32, 8)
    edge = round_up(-(-head_rows // lines), 16)
    new_master, new_one, new_two, new_weight = pl.pallas_call(
        functools.partial(final_kernel, even_size=even_size, head_rows=head_rows, chips=chips),
        out_shape=[state, state, state, struct((per, columns), bf16)],
        in_specs=[smem()] * 2 + [vmem()] * 8,
        out_specs=[anywhere(), anywhere(), anywhere(), vmem()],
        scratch_shapes=[
            pltpu.VMEM((sum_rows, LANES), f32),
            pltpu.VMEM((sum_rows, LANES), f32),
            pltpu.VMEM((round_up(flat_rows + head_rows + 32, 8), LANES), f32),
            pltpu.VMEM((bucket_rows, LANES), f32),
            pltpu.VMEM((bucket_rows, LANES), f32),
            pltpu.VMEM((edge * lines + 2 * head_rows + 32, LANES), f32),
            pltpu.SemaphoreType.DMA((4, 3)),
        ],
        compiler_params=params(32),
        cost_estimate=cost(4 * rows * kept * columns, 25_000_000),
        name="final",
    )(
        position,
        offsets,
        turned,
        total[0],
        heads,
        *last,
        old,
        first,
        second,
    )
    return (
        new_master.reshape(1, 1, bucket_cap),
        new_one.reshape(1, 1, bucket_cap),
        new_two.reshape(1, 1, bucket_cap),
        new_weight[None],
        router_grad.reshape(token_count, 1),
    )


def solution(mesh):
    placed = (
        P(("dp", "expert"), None),
        P(("dp", "expert"), None),
        P(("dp", "expert"), None, None),
        P(("dp", "expert"), None),
        P(("dp", "expert"), None),
        P("expert", "dp", None),
        P("expert", "dp", None),
        P("expert", "dp", None),
        P("expert", "dp", None),
        P(),
    )
    return jax.shard_map(
        shards,
        mesh=mesh,
        in_specs=placed,
        out_specs=(
            P("expert", "dp", None),
            P("expert", "dp", None),
            P("expert", "dp", None),
            P("expert", "dp", None),
            P(("dp", "expert"), None),
        ),
        check_vma=False,
    )
```

profile of v0, /device:TPU:0, one launch (start us, length us, event | category | flops | bytes accessed | tf_op | source)
XLA Modules:
  0.0 139.2 jit_solution(12207528047075885508)
XLA Ops:
  0.6 3.1 %collective-permute-start = (bf16[96,2560]{1,0:T(8,128)(2,1)}, bf16[96,2560]{1,0:T(8,128)(2,1)}, u32[]{:S(2)}, u32[]{:S(2)}) collective-permute-start(bf16[96,2560]{1,0:T(8,128)(2,1)} %bitcast.21), channel_id=1, source_target_pairs={{0,8},{4,12},{8,16},{12,20},{16,24},{20,28},{24,0},{28,4},{1,9},{5... | collective-permute-start | bytes 1474568 | tf_op jit(solution)/shard_map/ppermute | solution.py:430
  7.1 1.8 %pack.1 = (f32[256,128]{1,0:T(8,128)S(1)}, f32[1,128]{1,0:T(1,128)S(1)}, bf16[4,64,4224]{2,1,0:T(8,128)(2,1)S(1)}) custom-call(s32[1,128]{1,0:T(1,128)S(1)} %bitcast.25, bf16[1,128]{1,0:T(2,128)(2,1)S(1)} %bitcast.26, bf16[128,2560]{1,0:T(8,128)(2,1)S(1)} %copy-done.4, bf16[128,1536]{1,0:T(8,128)(2,1)S(1)} %bitcast.24), custom_call_target="tpu_custom_call" | custom-call | bytes 6000000 | tf_op jit(solution)/shard_map/pack/pallas_call | solution.py:442
  10.9 3.8 %all-to-all-start.1 = ((bf16[4,64,4224]{2,1,0:T(8,128)(2,1)}), bf16[4,64,4224]{2,1,0:T(8,128)(2,1)S(1)}, u32[]{:S(2)}, u32[]{:S(2)}) async-start(bf16[4,64,4224]{2,1,0:T(8,128)(2,1)} %copy-done.3), calls=%async_computation.1 | async-start | bytes 4325376 | tf_op jit(solution)/shard_map/all_to_all | solution.py:436
  15.9 1.4 collective-permute-done.refs_2_
  20.1 12.8 %collective-permute-done.1.refs_4_ = bf16[96,2560]{1,0:T(8,128)(2,1)S(1)} collective-permute-done((bf16[96,2560]{1,0:T(8,128)(2,1)}, bf16[96,2560]{1,0:T(8,128)(2,1)S(1)}, u32[]{:S(2)}, u32[]{:S(2)}) %collective-permute-start.1) | collective-permute-done | bytes 491552 | tf_op jit(solution)/shard_map/ppermute | solution.py:430
  35.6 12.9 %collective-permute-done.4.refs_6_ = bf16[96,2560]{1,0:T(8,128)(2,1)} collective-permute-done((bf16[96,2560]{1,0:T(8,128)(2,1)S(1)}, bf16[96,2560]{1,0:T(8,128)(2,1)}, u32[]{:S(2)}, u32[]{:S(2)}) %collective-permute-start.4) | collective-permute-done | bytes 491552 | tf_op jit(solution)/shard_map/ppermute | solution.py:430
  48.5 3.5 %all-to-all-start = ((bf16[8,128,384]{2,1,0:T(8,128)(2,1)}), bf16[8,128,384]{2,1,0:T(8,128)(2,1)S(1)}, u32[]{:S(2)}, u32[]{:S(2)}) async-start(bf16[8,128,384]{2,1,0:T(8,128)(2,1)} %window.1), calls=%async_computation | async-start | bytes 1572864 | tf_op jit(solution)/shard_map/all_to_all | solution.py:436
  53.7 4.8 %rows.1 = (bf16[256,1536]{1,0:T(8,128)(2,1)}, f32[256,128]{1,0:T(8,128)S(1)}) custom-call(s32[1]{0:T(128)} %bitcast.position_ref, bf16[256,2560]{1,0:T(8,128)(2,1)S(1)} %get-tuple-element.43.grads_ref, f32[256,768]{1,0:T(8,128)S(1)} %get-tuple-element.44.gate_factor, f32[256,768]{1,0:T(8,128)S(1)} %get-tuple-element.45.up_factor, ...), custom_call_target="tpu_custom_call" | custom-call | flops 1006632960 | bytes 8000000 | tf_op jit(solution)/shard_map/rows/pallas_call | solution.py:511
  58.4 2.0 %collective-permute-start.7 = (bf16[256,1536]{1,0:T(8,128)(2,1)}, bf16[256,1536]{1,0:T(8,128)(2,1)}, u32[]{:S(2)}, u32[]{:S(2)}) collective-permute-start(bf16[256,1536]{1,0:T(8,128)(2,1)} %get-tuple-element.52.refs_0_), channel_id=1, source_target_pairs={{0,8},{4,12},{8,16},{12,20},{16,24},{20,28},{24,0},{28,4},{1,9},{5... | collective-permute-start | bytes 2359304 | tf_op jit(solution)/shard_map/ppermute | solution.py:430
  60.4 26.3 %collective-permute-done.7.refs_2_ = bf16[256,1536]{1,0:T(8,128)(2,1)} collective-permute-done((bf16[256,1536]{1,0:T(8,128)(2,1)}, bf16[256,1536]{1,0:T(8,128)(2,1)}, u32[]{:S(2)}, u32[]{:S(2)}) %collective-permute-start.7) | collective-permute-done | bytes 786464 | tf_op jit(solution)/shard_map/ppermute | solution.py:430
  86.7 1.6 %collective-permute-start.8 = (bf16[256,1536]{1,0:T(8,128)(2,1)}, bf16[256,1536]{1,0:T(8,128)(2,1)}, u32[]{:S(2)}, u32[]{:S(2)}) collective-permute-start(bf16[256,1536]{1,0:T(8,128)(2,1)} %collective-permute-done.7.refs_2_), channel_id=1, source_target_pairs={{0,8},{4,12},{8,16},{12,20},{16,24},{20,28},{24,0},{28,4},{1,9},{5... | collective-permute-start | bytes 2359304 | tf_op jit(solution)/shard_map/ppermute | solution.py:430
  88.4 1.4 %all-to-all-done.windows_ref = bf16[8,128,384]{2,1,0:T(8,128)(2,1)S(1)} async-done(((bf16[8,128,384]{2,1,0:T(8,128)(2,1)}), bf16[8,128,384]{2,1,0:T(8,128)(2,1)S(1)}, u32[]{:S(2)}, u32[]{:S(2)}) %all-to-all-start) | async-done | bytes 786464 | tf_op jit(solution)/shard_map/all_to_all | solution.py:436
  89.8 1.8 %compact.1 = bf16[4,8,64,384]{3,2,1,0:T(8,128)(2,1)} custom-call(s32[1]{0:T(128)} %bitcast.position_ref, bf16[8,128,384]{2,1,0:T(8,128)(2,1)S(1)} %all-to-all-done.windows_ref, f32[256,128]{1,0:T(8,128)S(1)} %get-tuple-element.51.scores_ref), custom_call_target="tpu_custom_call" | custom-call | bytes 3000000 | tf_op jit(solution)/shard_map/compact/pallas_call | solution.py:378
  91.6 3.7 %all-to-all-start.2 = ((bf16[4,8,64,384]{3,2,1,0:T(8,128)(2,1)}), bf16[4,8,64,384]{3,2,1,0:T(8,128)(2,1)S(1)}, u32[]{:S(2)}, u32[]{:S(2)}) async-start(bf16[4,8,64,384]{3,2,1,0:T(8,128)(2,1)} %compact.1), calls=%async_computation.2 | async-start | bytes 3145728 | tf_op jit(solution)/shard_map/all_to_all | solution.py:436
  95.8 12.0 %collective-permute-done.8.refs_0_ = bf16[256,1536]{1,0:T(8,128)(2,1)} collective-permute-done((bf16[256,1536]{1,0:T(8,128)(2,1)}, bf16[256,1536]{1,0:T(8,128)(2,1)}, u32[]{:S(2)}, u32[]{:S(2)}) %collective-permute-start.8) | collective-permute-done | bytes 786464 | tf_op jit(solution)/shard_map/ppermute | solution.py:430
  108.2 1.6 %heads.1 = f32[3,120,128]{2,1,0:T(8,128)} custom-call(f32[3960,128]{1,0:T(8,128)} %bitcast.15, f32[3960,128]{1,0:T(8,128)} %bitcast.17, f32[3960,128]{1,0:T(8,128)} %bitcast.19), custom_call_target="tpu_custom_call" | custom-call | bytes 400000 | tf_op jit(solution)/shard_map/heads/pallas_call | solution.py:528
  109.8 1.4 %collective-permute-start.13 = (f32[3,120,128]{2,1,0:T(8,128)}, f32[3,120,128]{2,1,0:T(8,128)S(1)}, u32[]{:S(2)}, u32[]{:S(2)}) collective-permute-start(f32[3,120,128]{2,1,0:T(8,128)} %heads.1), channel_id=1, source_target_pairs={{4,0},{8,4},{12,8},{16,12},{20,16},{24,20},{28,24},{5,1},{9,5},{13... | collective-permute-start | bytes 552968 | tf_op jit(solution)/shard_map/ppermute | solution.py:538
  111.2 3.3 %all-to-all-done.2.rows_ref = bf16[4,8,64,384]{3,2,1,0:T(8,128)(2,1)S(1)} async-done(((bf16[4,8,64,384]{3,2,1,0:T(8,128)(2,1)}), bf16[4,8,64,384]{3,2,1,0:T(8,128)(2,1)S(1)}, u32[]{:S(2)}, u32[]{:S(2)}) %all-to-all-start.2) | async-done | bytes 1572896 | tf_op jit(solution)/shard_map/all_to_all | solution.py:436
  115.6 3.1 %early1.1.refs_2_ = f32[336,1536]{1,0:T(8,128)S(1)} custom-call(s32[1]{0:T(128)} %bitcast.position_ref, bf16[8,336,256]{2,1,0:T(8,128)(2,1)S(1)} %turn.1.turned_ref, bf16[256,1536]{1,0:T(8,128)(2,1)} %get-tuple-element.52.refs_0_, bf16[256,1536]{1,0:T(8,128)(2,1)} %collective-permute-done.11.refs_1_, bf16[256,1536]{1,0:T(8,128)(2,1)} %collective-permute-done.7.refs_2_, ...), custom_call_target="tpu_custom_call" | custom-call | flops 1056964608 | bytes 8000000 | tf_op jit(solution)/shard_map/early1/pallas_call | solution.py:378
  118.8 2.0 %early2.1.early_ref = f32[336,1536]{1,0:T(8,128)S(1)} custom-call(s32[1]{0:T(128)} %bitcast.position_ref, bf16[8,336,256]{2,1,0:T(8,128)(2,1)S(1)} %turn.1.turned_ref, bf16[256,1536]{1,0:T(8,128)(2,1)} %collective-permute-done.8.refs_0_, bf16[256,1536]{1,0:T(8,128)(2,1)S(1)} %collective-permute-done.10.refs_1_, f32[336,1536]{1,0:T(8,128)S(1)} %early1.1.refs_2_), custom_call_target="tpu_custom_call" | custom-call | flops 528482304 | bytes 8000000 | tf_op jit(solution)/shard_map/early2/pallas_call | solution.py:378
  120.8 9.2 %collective-permute-done.9.own_ref = bf16[256,1536]{1,0:T(8,128)(2,1)S(1)} collective-permute-done((bf16[256,1536]{1,0:T(8,128)(2,1)}, bf16[256,1536]{1,0:T(8,128)(2,1)S(1)}, u32[]{:S(2)}, u32[]{:S(2)}) %collective-permute-start.9) | collective-permute-done | bytes 786464 | tf_op jit(solution)/shard_map/ppermute | solution.py:430
  130.0 1.6 %collective-permute-start.14 = (bf16[256,1536]{1,0:T(8,128)(2,1)S(1)}, bf16[256,1536]{1,0:T(8,128)(2,1)S(1)}, u32[]{:S(2)}, u32[]{:S(2)}) collective-permute-start(bf16[256,1536]{1,0:T(8,128)(2,1)S(1)} %collective-permute-done.9.own_ref), channel_id=1, source_target_pairs={{0,4},{4,0},{8,12},{12,8},{16,20},{20,16},{24,28},{28,24},{1,5},{5... | collective-permute-start | bytes 2359304 | tf_op jit(solution)/shard_map/ppermute | solution.py:433
  131.6 1.9 %collective-permute-done.14.other_ref = bf16[256,1536]{1,0:T(8,128)(2,1)S(1)} collective-permute-done((bf16[256,1536]{1,0:T(8,128)(2,1)S(1)}, bf16[256,1536]{1,0:T(8,128)(2,1)S(1)}, u32[]{:S(2)}, u32[]{:S(2)}) %collective-permute-start.14) | collective-permute-done | bytes 786464 | tf_op jit(solution)/shard_map/ppermute | solution.py:433
  133.5 5.7 %final.1 = (f32[3960,128]{1,0:T(8,128)}, f32[3960,128]{1,0:T(8,128)}, f32[3960,128]{1,0:T(8,128)}, bf16[320,1536]{1,0:T(8,128)(2,1)}) custom-call(s32[1]{0:T(128)} %bitcast.position_ref, s32[9]{0:T(128)S(1)} %copy-done.21, bf16[8,336,256]{2,1,0:T(8,128)(2,1)S(1)} %turn.1.turned_ref, f32[336,1536]{1,0:T(8,128)S(1)} %early2.1.early_ref, ...), custom_call_target="tpu_custom_call" | custom-call | flops 528482304 | bytes 25000000 | tf_op jit(solution)/shard_map/final/pallas_call | solution.py:597
  (68 shorter events, 15.6 us)
Async XLA Ops:
  0.6 16.6 %collective-permute-start = (bf16[96,2560]{1,0:T(8,128)(2,1)}, bf16[96,2560]{1,0:T(8,128)(2,1)}, u32[]{:S(2)}, u32[]{:S(2)}) collective-permute-start(bf16[96,2560]{1,0:T(8,128)(2,1)} %bitcast.21), channel_id=1, source_target_pairs={{0,8},{4,12},{8,16},{12,20},{16,24},{20,28},{24,0},{28,4},{1,9},{5... | collective-permute-start | bytes 1474568 | tf_op jit(solution)/shard_map/ppermute | solution.py:430
  10.9 3.9 %copy-start.5 = (bf16[128,2560]{1,0:T(8,128)(2,1)S(1)}, bf16[128,2560]{1,0:T(8,128)(2,1)}, u32[]{:S(2)}) copy-start(bf16[128,2560]{1,0:T(8,128)(2,1)} %tokens_ref.1) | copy-start | bytes 1966084
  10.9 37.5 %all-to-all-start.1 = ((bf16[4,64,4224]{2,1,0:T(8,128)(2,1)}), bf16[4,64,4224]{2,1,0:T(8,128)(2,1)S(1)}, u32[]{:S(2)}, u32[]{:S(2)}) async-start(bf16[4,64,4224]{2,1,0:T(8,128)(2,1)} %copy-done.3), calls=%async_computation.1 | async-start | bytes 4325376 | tf_op jit(solution)/shard_map/all_to_all | solution.py:436
  14.8 3.2 %collective-permute-start.2 = (bf16[96,2560]{1,0:T(8,128)(2,1)S(1)}, bf16[96,2560]{1,0:T(8,128)(2,1)S(1)}, u32[]{:S(2)}, u32[]{:S(2)}) collective-permute-start(bf16[96,2560]{1,0:T(8,128)(2,1)S(1)} %bitcast.22), channel_id=1, source_target_pairs={{0,4},{4,0},{8,12},{12,8},{16,20},{20,16},{24,28},{28,24},{1,5},{5... | collective-permute-start | bytes 1474568 | tf_op jit(solution)/shard_map/ppermute | solution.py:433
  17.3 2.1 %collective-permute-start.3 = (bf16[96,2560]{1,0:T(8,128)(2,1)}, bf16[96,2560]{1,0:T(8,128)(2,1)S(1)}, u32[]{:S(2)}, u32[]{:S(2)}) collective-permute-start(bf16[96,2560]{1,0:T(8,128)(2,1)} %collective-permute-done.refs_2_), channel_id=1, source_target_pairs={{0,4},{4,0},{8,12},{12,8},{16,20},{20,16},{24,28},{28,24},{1,5},{5... | collective-permute-start | bytes 1474568 | tf_op jit(solution)/shard_map/ppermute | solution.py:433
  17.3 15.6 %collective-permute-start.1 = (bf16[96,2560]{1,0:T(8,128)(2,1)}, bf16[96,2560]{1,0:T(8,128)(2,1)S(1)}, u32[]{:S(2)}, u32[]{:S(2)}) collective-permute-start(bf16[96,2560]{1,0:T(8,128)(2,1)} %collective-permute-done.refs_2_), channel_id=1, source_target_pairs={{0,8},{4,12},{8,16},{12,20},{16,24},{20,28},{24,0},{28,4},{1,9},{5... | collective-permute-start | bytes 1474568 | tf_op jit(solution)/shard_map/ppermute | solution.py:430
  32.9 1.9 %collective-permute-start.5 = (bf16[96,2560]{1,0:T(8,128)(2,1)S(1)}, bf16[96,2560]{1,0:T(8,128)(2,1)S(1)}, u32[]{:S(2)}, u32[]{:S(2)}) collective-permute-start(bf16[96,2560]{1,0:T(8,128)(2,1)S(1)} %collective-permute-done.1.refs_4_), channel_id=1, source_target_pairs={{0,4},{4,0},{8,12},{12,8},{16,20},{20,16},{24,28},{28,24},{1,5},{5... | collective-permute-start | bytes 1474568 | tf_op jit(solution)/shard_map/ppermute | solution.py:433
  32.9 15.5 %collective-permute-start.4 = (bf16[96,2560]{1,0:T(8,128)(2,1)S(1)}, bf16[96,2560]{1,0:T(8,128)(2,1)}, u32[]{:S(2)}, u32[]{:S(2)}) collective-permute-start(bf16[96,2560]{1,0:T(8,128)(2,1)S(1)} %collective-permute-done.1.refs_4_), channel_id=1, source_target_pairs={{0,8},{4,12},{8,16},{12,20},{16,24},{20,28},{24,0},{28,4},{1,9},{5... | collective-permute-start | bytes 1474568 | tf_op jit(solution)/shard_map/ppermute | solution.py:430
  48.5 4.4 %collective-permute-start.6 = (bf16[96,2560]{1,0:T(8,128)(2,1)}, bf16[96,2560]{1,0:T(8,128)(2,1)S(1)}, u32[]{:S(2)}, u32[]{:S(2)}) collective-permute-start(bf16[96,2560]{1,0:T(8,128)(2,1)} %collective-permute-done.4.refs_6_), channel_id=1, source_target_pairs={{0,4},{4,0},{8,12},{12,8},{16,20},{20,16},{24,28},{28,24},{1,5},{5... | collective-permute-start | bytes 1474568 | tf_op jit(solution)/shard_map/ppermute | solution.py:433
  48.5 41.3 %all-to-all-start = ((bf16[8,128,384]{2,1,0:T(8,128)(2,1)}), bf16[8,128,384]{2,1,0:T(8,128)(2,1)S(1)}, u32[]{:S(2)}, u32[]{:S(2)}) async-start(bf16[8,128,384]{2,1,0:T(8,128)(2,1)} %window.1), calls=%async_computation | async-start | bytes 1572864 | tf_op jit(solution)/shard_map/all_to_all | solution.py:436
  58.4 28.3 %collective-permute-start.7 = (bf16[256,1536]{1,0:T(8,128)(2,1)}, bf16[256,1536]{1,0:T(8,128)(2,1)}, u32[]{:S(2)}, u32[]{:S(2)}) collective-permute-start(bf16[256,1536]{1,0:T(8,128)(2,1)} %get-tuple-element.52.refs_0_), channel_id=1, source_target_pairs={{0,8},{4,12},{8,16},{12,20},{16,24},{20,28},{24,0},{28,4},{1,9},{5... | collective-permute-start | bytes 2359304 | tf_op jit(solution)/shard_map/ppermute | solution.py:430
  86.7 21.1 %collective-permute-start.8 = (bf16[256,1536]{1,0:T(8,128)(2,1)}, bf16[256,1536]{1,0:T(8,128)(2,1)}, u32[]{:S(2)}, u32[]{:S(2)}) collective-permute-start(bf16[256,1536]{1,0:T(8,128)(2,1)} %collective-permute-done.7.refs_2_), channel_id=1, source_target_pairs={{0,8},{4,12},{8,16},{12,20},{16,24},{20,28},{24,0},{28,4},{1,9},{5... | collective-permute-start | bytes 2359304 | tf_op jit(solution)/shard_map/ppermute | solution.py:430
  91.6 22.9 %all-to-all-start.2 = ((bf16[4,8,64,384]{3,2,1,0:T(8,128)(2,1)}), bf16[4,8,64,384]{3,2,1,0:T(8,128)(2,1)S(1)}, u32[]{:S(2)}, u32[]{:S(2)}) async-start(bf16[4,8,64,384]{3,2,1,0:T(8,128)(2,1)} %compact.1), calls=%async_computation.2 | async-start | bytes 3145728 | tf_op jit(solution)/shard_map/all_to_all | solution.py:436
  95.3 20.3 %collective-permute-start.11 = (bf16[256,1536]{1,0:T(8,128)(2,1)}, bf16[256,1536]{1,0:T(8,128)(2,1)}, u32[]{:S(2)}, u32[]{:S(2)}) collective-permute-start(bf16[256,1536]{1,0:T(8,128)(2,1)} %get-tuple-element.52.refs_0_), channel_id=1, source_target_pairs={{0,4},{4,0},{8,12},{12,8},{16,20},{20,16},{24,28},{28,24},{1,5},{5... | collective-permute-start | bytes 2359304 | tf_op jit(solution)/shard_map/ppermute | solution.py:433
  95.3 20.3 %collective-permute-start.12 = (bf16[256,1536]{1,0:T(8,128)(2,1)}, bf16[256,1536]{1,0:T(8,128)(2,1)}, u32[]{:S(2)}, u32[]{:S(2)}) collective-permute-start(bf16[256,1536]{1,0:T(8,128)(2,1)} %collective-permute-done.7.refs_2_), channel_id=1, source_target_pairs={{0,4},{4,0},{8,12},{12,8},{16,20},{20,16},{24,28},{28,24},{1,5},{5... | collective-permute-start | bytes 2359304 | tf_op jit(solution)/shard_map/ppermute | solution.py:433
  107.9 10.9 %collective-permute-start.10 = (bf16[256,1536]{1,0:T(8,128)(2,1)}, bf16[256,1536]{1,0:T(8,128)(2,1)S(1)}, u32[]{:S(2)}, u32[]{:S(2)}) collective-permute-start(bf16[256,1536]{1,0:T(8,128)(2,1)} %collective-permute-done.8.refs_0_), channel_id=1, source_target_pairs={{0,4},{4,0},{8,12},{12,8},{16,20},{20,16},{24,28},{28,24},{1,5},{5... | collective-permute-start | bytes 2359304 | tf_op jit(solution)/shard_map/ppermute | solution.py:433
  107.9 22.1 %collective-permute-start.9 = (bf16[256,1536]{1,0:T(8,128)(2,1)}, bf16[256,1536]{1,0:T(8,128)(2,1)S(1)}, u32[]{:S(2)}, u32[]{:S(2)}) collective-permute-start(bf16[256,1536]{1,0:T(8,128)(2,1)} %collective-permute-done.8.refs_0_), channel_id=1, source_target_pairs={{0,8},{4,12},{8,16},{12,20},{16,24},{20,28},{24,0},{28,4},{1,9},{5... | collective-permute-start | bytes 2359304 | tf_op jit(solution)/shard_map/ppermute | solution.py:430
  109.8 5.1 %copy-start.18 = (f32[256,128]{1,0:T(8,128)S(1)}, f32[256,128]{1,0:T(8,128)}, u32[]{:S(2)}) copy-start(f32[256,128]{1,0:T(8,128)} %copy-done.17) | copy-start | bytes 393220
  109.8 11.1 %collective-permute-start.13 = (f32[3,120,128]{2,1,0:T(8,128)}, f32[3,120,128]{2,1,0:T(8,128)S(1)}, u32[]{:S(2)}, u32[]{:S(2)}) collective-permute-start(f32[3,120,128]{2,1,0:T(8,128)} %heads.1), channel_id=1, source_target_pairs={{4,0},{8,4},{12,8},{16,12},{20,16},{24,20},{28,24},{5,1},{9,5},{13... | collective-permute-start | bytes 552968 | tf_op jit(solution)/shard_map/ppermute | solution.py:538
  118.7 14.8 %copy-start = (f32[1,1,506880]{2,1,0:T(1,128)S(1)}, f32[1,1,506880]{2,1,0:T(1,128)}, u32[]{:S(2)}) copy-start(f32[1,1,506880]{2,1,0:T(1,128)} %param.16) | copy-start | bytes 6082564
  118.7 14.8 %copy-start.1 = (f32[1,1,506880]{2,1,0:T(1,128)S(1)}, f32[1,1,506880]{2,1,0:T(1,128)}, u32[]{:S(2)}) copy-start(f32[1,1,506880]{2,1,0:T(1,128)} %param.17) | copy-start | bytes 6082564
  118.8 14.8 %copy-start.2 = (f32[1,1,506880]{2,1,0:T(1,128)S(1)}, f32[1,1,506880]{2,1,0:T(1,128)}, u32[]{:S(2)}) copy-start(f32[1,1,506880]{2,1,0:T(1,128)} %param.18) | copy-start | bytes 6082564
  118.8 14.8 %copy-start.21 = (s32[9]{0:T(128)S(1)}, s32[9]{0:T(128)}, u32[]{:S(2)}) copy-start(s32[9]{0:T(128)} %offsets_ref.1) | copy-start | bytes 112
  130.0 3.6 %collective-permute-start.14 = (bf16[256,1536]{1,0:T(8,128)(2,1)S(1)}, bf16[256,1536]{1,0:T(8,128)(2,1)S(1)}, u32[]{:S(2)}, u32[]{:S(2)}) collective-permute-start(bf16[256,1536]{1,0:T(8,128)(2,1)S(1)} %collective-permute-done.9.own_ref), channel_id=1, source_target_pairs={{0,4},{4,0},{8,12},{12,8},{16,20},{20,16},{24,28},{28,24},{1,5},{5... | collective-permute-start | bytes 2359304 | tf_op jit(solution)/shard_map/ppermute | solution.py:433
  (16 other events, 18.9 us)
where the time goes:
time: 140 us; the launch traced here: 139 us
  waiting for transfers between devices  82.8 us (59%)
  Pallas kernels  23.8 us (17%)
  starting transfers between devices  22.4 us (16%)
  local copies, waits for them, and re-layouts  9.32 us (7%)
    ppermute x6, waiting for transfers between devices, onward(): lax.ppermute(block, 'dp', [(i, (i + 2) % parts) for i in range(parts)])  74.6 us
    all_to_all x3, starting transfers between devices, exchanged(): return lax.all_to_all(block, axis, split_axis=0, concat_axis=0, tiled=True)  11.1 us
    pallas_call x7, Pallas kernels, call(): pl.pallas_call(kernel, out_shape=outs, in_specs=[smem()] * len(scalars) +...  9.98 us
    unnamed x44, local copies, waits for them, and re-layouts  9.32 us
    ppermute x6, starting transfers between devices, onward(): lax.ppermute(block, 'dp', [(i, (i + 2) % parts) for i in range(parts)])  7.75 us
    pallas_call x1, Pallas kernels, shards(): pl.pallas_call(functools.partial(final_kernel, even_size=even_size, head_...  5.7 us
    pallas_call x1, Pallas kernels, shards(): pl.pallas_call(functools.partial(row_kernel, chips=chips), out_shape=[str...  4.75 us
    all_to_all x3, waiting for transfers between devices, exchanged(): return lax.all_to_all(block, axis, split_axis=0, concat_axis=0, tiled=True)  4.68 us
  transfers between devices with their start and end apart: 18, of which 11 were waited for; matrix products, arithmetic and copies ran while one was open for 0% of the time, Pallas kernels for 13%

commit v1 on v0

--- a/solution.py
+++ b/solution.py
@@ -139,7 +139,7 @@
     gate_ref[...] = weight * (up * sig * (1.0 + gate * (1.0 - sig)))
 
 
-def row_kernel(position_ref, grads_ref, gate_factor, up_factor, score_factor, *refs, chips):
+def row_kernel(position_ref, grads_ref, gate_factor, up_factor, score_factor, *refs, chips, places):
     down_refs, refs = refs[:-6], refs[-5:]
     joined_any, scores_ref, joined, down, sems = refs
     hidden = down.shape[0]
@@ -149,8 +149,9 @@
         if size == hidden:
             at = 0
         else:
-            slab = lax.rem(position_ref[0] + 2 * (chips - n // 2), 2 * chips) ^ (n % 2)
-            at = pl.multiple_of(slab * size, 16)
+            k, other, half = places[n]
+            slab = lax.rem(position_ref[0] + 2 * (chips - k), 2 * chips) ^ other
+            at = pl.multiple_of(slab * (hidden // (2 * chips)) + half * size, 16)
         loads.append(pltpu.make_async_copy(down_ref, down.at[pl.ds(at, size)], sems.at[n]))
     for load in loads:
         load.start()
@@ -454,7 +455,7 @@
             pltpu.VMEM((experts, cap, wide), bf16),
             pltpu.SemaphoreType.DMA((2 + experts,)),
         ],
-        compiler_params=params(16),
+        compiler_params=params(60),
         cost_estimate=cost(0, 6_000_000),
         name="pack",
     )(
@@ -472,22 +473,27 @@
         12,
         moved=2_000_000,
     )
-    if down_weight.shape[1] % 16 == 0:
-        held, other = [down_weight[0]], [swapped(down_weight[0])]
+    size = down_weight.shape[1] // 2
+    if size % 16 == 0:
+        places = [(0, 0, 0), (0, 1, 0)]
+        other = [swapped(down_weight[0])]
+        down = [down_weight[0], other[0]]
+        blocks = [down_weight[0, :size], down_weight[0, size:]]
         for k in range(1, chips):
-            arrival = onward(held[-1])
+            blocks = [onward(block) for block in blocks]
             if k == 1:
-                arrival, windows = tied(arrival, windows)
+                blocks[0], blocks[1], windows = tied(*blocks, windows)
             else:
-                arrival, other = tied(arrival, other)
-            held.append(arrival)
-            other.append(swapped(arrival))
+                blocks[1], other = tied(blocks[1], other)
             if k == chips - 1:
-                windows, held[-1] = tied(windows, held[-1])
-        down = [piece for pair in zip(held, other) for piece in pair]
+                windows, blocks[0] = tied(windows, blocks[0])
+            other = [swapped(block) for block in blocks]
+            down += blocks + other
+            places += [(k, o, h) for o in (0, 1) for h in (0, 1)]
     else:
         down = [lax.all_gather(down_weight, "dp", axis=1, tiled=True)[0]]
         windows, down[0] = tied(windows, down[0])
+        places = None
     arrived = exchanged(packed, "expert").reshape(rows, wide)
     windows = exchanged(windows, "dp")
     factors = call(
@@ -509,7 +515,7 @@
         name="ready",
     )(down[-1])
     joined, scores = pl.pallas_call(
-        functools.partial(row_kernel, chips=chips),
+        functools.partial(row_kernel, chips=chips, places=places),
         out_shape=[struct((rows, columns), bf16), struct((rows, LANES), f32)],
         in_specs=[smem()] + [vmem()] * 4 + [anywhere()] * (len(down) + 1),
         out_specs=[hbm(), vmem()],

time: 140 us -> 148 us (1.057)
  Pallas kernels: 23.8 us -> 28.4 us
  waiting for transfers between devices: 82.8 us -> 86 us
  starting transfers between devices: 22.4 us -> 25.5 us
  local copies, waits for them, and re-layouts: 9.32 us -> 6.36 us
    ppermute x6 -> x9, waiting for transfers between devices: 74.6 us -> 79.3 us  [onward(): lax.ppermute(block, 'dp', [(i, (i + 2) % parts) for i in range(parts)])]
    unnamed x44 -> x48, local copies, waits for them, and re-layouts: 9.32 us -> 6.33 us
    pallas_call x1, Pallas kernels: 1.8 us -> 4.59 us  [shards(): pl.pallas_call(pack_kernel, out_shape=[struct((rows, token_count), f32),...]
    pallas_call x1, Pallas kernels: 4.75 us -> 6.56 us  [shards(): pl.pallas_call(functools.partial(row_kernel, chips=chips, places=places),...]
    ppermute x8 -> x11, waiting for transfers between devices: 3.58 us -> 1.94 us  [swapped(): return lax.ppermute(block, 'dp', [(i, i ^ 1) for i in range(parts)])]
    all_to_all x3, starting transfers between devices: 11.1 us -> 12.7 us  [exchanged(): return lax.all_to_all(block, axis, split_axis=0, concat_axis=0, tiled=True)]
    ppermute x8 -> x11, starting transfers between devices: 2.16 us -> 3.18 us  [swapped(): return lax.ppermute(block, 'dp', [(i, i ^ 1) for i in range(parts)])]
    ppermute x6 -> x9, starting transfers between devices: 7.75 us -> 8.16 us  [onward(): lax.ppermute(block, 'dp', [(i, (i + 2) % parts) for i in range(parts)])]
  transfers between devices with their start and end apart: 18 -> 24, of which waited for: 11 -> 12; matrix products, arithmetic and copies ran while one was open for 0% -> 0% of each run, Pallas kernels for 13% -> 12%
where the time goes in v1:
time: 148 us; the launch traced here: 147 us
  waiting for transfers between devices  86 us (58%)
  Pallas kernels  28.4 us (19%)
  starting transfers between devices  25.5 us (17%)
  local copies, waits for them, and re-layouts  6.36 us (4%)
    ppermute x9, waiting for transfers between devices, onward(): lax.ppermute(block, 'dp', [(i, (i + 2) % parts) for i in range(parts)])  79.3 us
    all_to_all x3, starting transfers between devices, exchanged(): return lax.all_to_all(block, axis, split_axis=0, concat_axis=0, tiled=True)  12.7 us
    pallas_call x7, Pallas kernels, call(): pl.pallas_call(kernel, out_shape=outs, in_specs=[smem()] * len(scalars) +...  10 us
    ppermute x9, starting transfers between devices, onward(): lax.ppermute(block, 'dp', [(i, (i + 2) % parts) for i in range(parts)])  8.16 us
    pallas_call x1, Pallas kernels, shards(): pl.pallas_call(functools.partial(row_kernel, chips=chips, places=places),...  6.56 us
    unnamed x48, local copies, waits for them, and re-layouts  6.33 us
    pallas_call x1, Pallas kernels, shards(): pl.pallas_call(functools.partial(final_kernel, even_size=even_size, head_...  5.72 us
    all_to_all x3, waiting for transfers between devices, exchanged(): return lax.all_to_all(block, axis, split_axis=0, concat_axis=0, tiled=True)  4.73 us
  transfers between devices with their start and end apart: 24, of which 12 were waited for; matrix products, arithmetic and copies ran while one was open for 0% of the time, Pallas kernels for 12%

profile of v1, /device:TPU:0, one launch (start us, length us, event | category | flops | bytes accessed | tf_op | source)
XLA Modules:
  0.0 147.2 jit_solution(102871527434610211)
XLA Ops:
  0.6 4.6 %pack.1 = (f32[256,128]{1,0:T(8,128)}, f32[1,128]{1,0:T(1,128)}, bf16[4,64,4224]{2,1,0:T(8,128)(2,1)}) custom-call(s32[1,128]{1,0:T(1,128)} %bitcast.28, bf16[1,128]{1,0:T(2,128)(2,1)} %bitcast.29, bf16[128,2560]{1,0:T(8,128)(2,1)} %grads_any.1, bf16[128,1536]{1,0:T(8,128)(2,1)} %bitcast.27), custom_call_target="tpu_custom_call" | custom-call | bytes 6000000 | tf_op jit(solution)/shard_map/pack/pallas_call | solution.py:443
  5.3 5.3 %all-to-all-start.1 = ((bf16[4,64,4224]{2,1,0:T(8,128)(2,1)}), bf16[4,64,4224]{2,1,0:T(8,128)(2,1)S(1)}, u32[]{:S(2)}, u32[]{:S(2)}) async-start(bf16[4,64,4224]{2,1,0:T(8,128)(2,1)} %get-tuple-element.34), calls=%async_computation.1 | async-start | bytes 4325376 | tf_op jit(solution)/shard_map/all_to_all | solution.py:437
  10.6 1.6 %collective-permute-start.1 = (bf16[48,2560]{1,0:T(8,128)(2,1)S(1)}, bf16[48,2560]{1,0:T(8,128)(2,1)S(1)}, u32[]{:S(2)}, u32[]{:S(2)}) collective-permute-start(bf16[48,2560]{1,0:T(8,128)(2,1)S(1)} %get-tuple-element.55), channel_id=1, source_target_pairs={{0,8},{4,12},{8,16},{12,20},{16,24},{20,28},{24,0},{28,4},{1,9},{5... | collective-permute-start | bytes 737288 | tf_op jit(solution)/shard_map/ppermute | solution.py:431
  14.9 6.4 %collective-permute-done.1.refs_3_ = bf16[48,2560]{1,0:T(8,128)(2,1)S(1)} collective-permute-done((bf16[48,2560]{1,0:T(8,128)(2,1)S(1)}, bf16[48,2560]{1,0:T(8,128)(2,1)S(1)}, u32[]{:S(2)}, u32[]{:S(2)}) %collective-permute-start.1) | collective-permute-done | bytes 245792 | tf_op jit(solution)/shard_map/ppermute | solution.py:431
  21.3 4.1 %collective-permute-done.refs_2_ = bf16[48,2560]{1,0:T(8,128)(2,1)S(1)} collective-permute-done((bf16[48,2560]{1,0:T(8,128)(2,1)S(1)}, bf16[48,2560]{1,0:T(8,128)(2,1)S(1)}, u32[]{:S(2)}, u32[]{:S(2)}) %collective-permute-start) | collective-permute-done | bytes 245792 | tf_op jit(solution)/shard_map/ppermute | solution.py:431
  29.0 6.9 %collective-permute-done.7.refs_7_ = bf16[48,2560]{1,0:T(8,128)(2,1)S(1)} collective-permute-done((bf16[48,2560]{1,0:T(8,128)(2,1)S(1)}, bf16[48,2560]{1,0:T(8,128)(2,1)S(1)}, u32[]{:S(2)}, u32[]{:S(2)}) %collective-permute-start.7) | collective-permute-done | bytes 245792 | tf_op jit(solution)/shard_map/ppermute | solution.py:431
  36.7 4.2 %collective-permute-done.2.refs_6_ = bf16[48,2560]{1,0:T(8,128)(2,1)S(1)} collective-permute-done((bf16[48,2560]{1,0:T(8,128)(2,1)S(1)}, bf16[48,2560]{1,0:T(8,128)(2,1)S(1)}, u32[]{:S(2)}, u32[]{:S(2)}) %collective-permute-start.2) | collective-permute-done | bytes 245792 | tf_op jit(solution)/shard_map/ppermute | solution.py:431
  43.5 8.0 %collective-permute-done.10.refs_11_ = bf16[48,2560]{1,0:T(8,128)(2,1)} collective-permute-done((bf16[48,2560]{1,0:T(8,128)(2,1)S(1)}, bf16[48,2560]{1,0:T(8,128)(2,1)}, u32[]{:S(2)}, u32[]{:S(2)}) %collective-permute-start.10) | collective-permute-done | bytes 245792 | tf_op jit(solution)/shard_map/ppermute | solution.py:431
  52.2 4.2 %collective-permute-done.3.refs_10_ = bf16[48,2560]{1,0:T(8,128)(2,1)} collective-permute-done((bf16[48,2560]{1,0:T(8,128)(2,1)S(1)}, bf16[48,2560]{1,0:T(8,128)(2,1)}, u32[]{:S(2)}, u32[]{:S(2)}) %collective-permute-start.3) | collective-permute-done | bytes 245792 | tf_op jit(solution)/shard_map/ppermute | solution.py:431
  56.4 3.5 %all-to-all-start = ((bf16[8,128,384]{2,1,0:T(8,128)(2,1)}), bf16[8,128,384]{2,1,0:T(8,128)(2,1)S(1)}, u32[]{:S(2)}, u32[]{:S(2)}) async-start(bf16[8,128,384]{2,1,0:T(8,128)(2,1)} %window.1), calls=%async_computation | async-start | bytes 1572864 | tf_op jit(solution)/shard_map/all_to_all | solution.py:437
  61.6 6.6 %rows.1 = (bf16[256,1536]{1,0:T(8,128)(2,1)}, f32[256,128]{1,0:T(8,128)S(1)}) custom-call(s32[1]{0:T(128)} %bitcast.position_ref, bf16[256,2560]{1,0:T(8,128)(2,1)S(1)} %get-tuple-element.35.grads_ref, f32[256,768]{1,0:T(8,128)S(1)} %get-tuple-element.36.gate_factor, f32[256,768]{1,0:T(8,128)S(1)} %get-tuple-element.37.up_factor, ...), custom_call_target="tpu_custom_call" | custom-call | flops 1006632960 | bytes 8000000 | tf_op jit(solution)/shard_map/rows/pallas_call | solution.py:517
  68.2 2.0 %collective-permute-start.13 = (bf16[256,1536]{1,0:T(8,128)(2,1)}, bf16[256,1536]{1,0:T(8,128)(2,1)}, u32[]{:S(2)}, u32[]{:S(2)}) collective-permute-start(bf16[256,1536]{1,0:T(8,128)(2,1)} %get-tuple-element.44.refs_0_), channel_id=1, source_target_pairs={{0,8},{4,12},{8,16},{12,20},{16,24},{20,28},{24,0},{28,4},{1,9},{5... | collective-permute-start | bytes 2359304 | tf_op jit(solution)/shard_map/ppermute | solution.py:431
  70.1 24.5 %collective-permute-done.13.refs_2_ = bf16[256,1536]{1,0:T(8,128)(2,1)} collective-permute-done((bf16[256,1536]{1,0:T(8,128)(2,1)}, bf16[256,1536]{1,0:T(8,128)(2,1)}, u32[]{:S(2)}, u32[]{:S(2)}) %collective-permute-start.13) | collective-permute-done | bytes 786464 | tf_op jit(solution)/shard_map/ppermute | solution.py:431
  94.6 1.6 %collective-permute-start.14 = (bf16[256,1536]{1,0:T(8,128)(2,1)}, bf16[256,1536]{1,0:T(8,128)(2,1)}, u32[]{:S(2)}, u32[]{:S(2)}) collective-permute-start(bf16[256,1536]{1,0:T(8,128)(2,1)} %collective-permute-done.13.refs_2_), channel_id=1, source_target_pairs={{0,8},{4,12},{8,16},{12,20},{16,24},{20,28},{24,0},{28,4},{1,9},{5... | collective-permute-start | bytes 2359304 | tf_op jit(solution)/shard_map/ppermute | solution.py:431
  97.7 1.8 %compact.1 = bf16[4,8,64,384]{3,2,1,0:T(8,128)(2,1)} custom-call(s32[1]{0:T(128)} %bitcast.position_ref, bf16[8,128,384]{2,1,0:T(8,128)(2,1)S(1)} %all-to-all-done.windows_ref, f32[256,128]{1,0:T(8,128)S(1)} %get-tuple-element.43.scores_ref), custom_call_target="tpu_custom_call" | custom-call | bytes 3000000 | tf_op jit(solution)/shard_map/compact/pallas_call | solution.py:379
  99.5 3.9 %all-to-all-start.2 = ((bf16[4,8,64,384]{3,2,1,0:T(8,128)(2,1)}), bf16[4,8,64,384]{3,2,1,0:T(8,128)(2,1)S(1)}, u32[]{:S(2)}, u32[]{:S(2)}) async-start(bf16[4,8,64,384]{3,2,1,0:T(8,128)(2,1)} %compact.1), calls=%async_computation.2 | async-start | bytes 3145728 | tf_op jit(solution)/shard_map/all_to_all | solution.py:437
  103.9 11.9 %collective-permute-done.14.refs_0_ = bf16[256,1536]{1,0:T(8,128)(2,1)} collective-permute-done((bf16[256,1536]{1,0:T(8,128)(2,1)}, bf16[256,1536]{1,0:T(8,128)(2,1)}, u32[]{:S(2)}, u32[]{:S(2)}) %collective-permute-start.14) | collective-permute-done | bytes 786464 | tf_op jit(solution)/shard_map/ppermute | solution.py:431
  119.1 3.3 %all-to-all-done.2.rows_ref = bf16[4,8,64,384]{3,2,1,0:T(8,128)(2,1)S(1)} async-done(((bf16[4,8,64,384]{3,2,1,0:T(8,128)(2,1)}), bf16[4,8,64,384]{3,2,1,0:T(8,128)(2,1)S(1)}, u32[]{:S(2)}, u32[]{:S(2)}) %all-to-all-start.2) | async-done | bytes 1572896 | tf_op jit(solution)/shard_map/all_to_all | solution.py:437
  123.6 3.1 %early1.1.refs_2_ = f32[336,1536]{1,0:T(8,128)S(1)} custom-call(s32[1]{0:T(128)} %bitcast.position_ref, bf16[8,336,256]{2,1,0:T(8,128)(2,1)S(1)} %turn.1.turned_ref, bf16[256,1536]{1,0:T(8,128)(2,1)} %get-tuple-element.44.refs_0_, bf16[256,1536]{1,0:T(8,128)(2,1)} %collective-permute-done.17.refs_1_, bf16[256,1536]{1,0:T(8,128)(2,1)} %collective-permute-done.13.refs_2_, ...), custom_call_target="tpu_custom_call" | custom-call | flops 1056964608 | bytes 8000000 | tf_op jit(solution)/shard_map/early1/pallas_call | solution.py:379
  126.8 2.0 %early2.1.early_ref = f32[336,1536]{1,0:T(8,128)S(1)} custom-call(s32[1]{0:T(128)} %bitcast.position_ref, bf16[8,336,256]{2,1,0:T(8,128)(2,1)S(1)} %turn.1.turned_ref, bf16[256,1536]{1,0:T(8,128)(2,1)} %collective-permute-done.14.refs_0_, bf16[256,1536]{1,0:T(8,128)(2,1)S(1)} %collective-permute-done.16.refs_1_, f32[336,1536]{1,0:T(8,128)S(1)} %early1.1.refs_2_), custom_call_target="tpu_custom_call" | custom-call | flops 528482304 | bytes 8000000 | tf_op jit(solution)/shard_map/early2/pallas_call | solution.py:379
  128.8 9.1 %collective-permute-done.15.own_ref = bf16[256,1536]{1,0:T(8,128)(2,1)S(1)} collective-permute-done((bf16[256,1536]{1,0:T(8,128)(2,1)}, bf16[256,1536]{1,0:T(8,128)(2,1)S(1)}, u32[]{:S(2)}, u32[]{:S(2)}) %collective-permute-start.15) | collective-permute-done | bytes 786464 | tf_op jit(solution)/shard_map/ppermute | solution.py:431
  137.9 1.6 %collective-permute-start.20 = (bf16[256,1536]{1,0:T(8,128)(2,1)S(1)}, bf16[256,1536]{1,0:T(8,128)(2,1)S(1)}, u32[]{:S(2)}, u32[]{:S(2)}) collective-permute-start(bf16[256,1536]{1,0:T(8,128)(2,1)S(1)} %collective-permute-done.15.own_ref), channel_id=1, source_target_pairs={{0,4},{4,0},{8,12},{12,8},{16,20},{20,16},{24,28},{28,24},{1,5},{5... | collective-permute-start | bytes 2359304 | tf_op jit(solution)/shard_map/ppermute | solution.py:434
  139.5 1.9 %collective-permute-done.20.other_ref = bf16[256,1536]{1,0:T(8,128)(2,1)S(1)} collective-permute-done((bf16[256,1536]{1,0:T(8,128)(2,1)S(1)}, bf16[256,1536]{1,0:T(8,128)(2,1)S(1)}, u32[]{:S(2)}, u32[]{:S(2)}) %collective-permute-start.20) | collective-permute-done | bytes 786464 | tf_op jit(solution)/shard_map/ppermute | solution.py:434
  141.5 5.7 %final.1 = (f32[3960,128]{1,0:T(8,128)}, f32[3960,128]{1,0:T(8,128)}, f32[3960,128]{1,0:T(8,128)}, bf16[320,1536]{1,0:T(8,128)(2,1)}) custom-call(s32[1]{0:T(128)} %bitcast.position_ref, s32[9]{0:T(128)S(1)} %copy-done.22, bf16[8,336,256]{2,1,0:T(8,128)(2,1)S(1)} %turn.1.turned_ref, f32[336,1536]{1,0:T(8,128)S(1)} %early2.1.early_ref, ...), custom_call_target="tpu_custom_call" | custom-call | flops 528482304 | bytes 25000000 | tf_op jit(solution)/shard_map/final/pallas_call | solution.py:603
  (85 shorter events, 18.3 us)
Async XLA Ops:
  5.3 51.1 %all-to-all-start.1 = ((bf16[4,64,4224]{2,1,0:T(8,128)(2,1)}), bf16[4,64,4224]{2,1,0:T(8,128)(2,1)S(1)}, u32[]{:S(2)}, u32[]{:S(2)}) async-start(bf16[4,64,4224]{2,1,0:T(8,128)(2,1)} %get-tuple-element.34), calls=%async_computation.1 | async-start | bytes 4325376 | tf_op jit(solution)/shard_map/all_to_all | solution.py:437
  10.6 10.7 %collective-permute-start.1 = (bf16[48,2560]{1,0:T(8,128)(2,1)S(1)}, bf16[48,2560]{1,0:T(8,128)(2,1)S(1)}, u32[]{:S(2)}, u32[]{:S(2)}) collective-permute-start(bf16[48,2560]{1,0:T(8,128)(2,1)S(1)} %get-tuple-element.55), channel_id=1, source_target_pairs={{0,8},{4,12},{8,16},{12,20},{16,24},{20,28},{24,0},{28,4},{1,9},{5... | collective-permute-start | bytes 737288 | tf_op jit(solution)/shard_map/ppermute | solution.py:431
  12.2 13.2 %collective-permute-start = (bf16[48,2560]{1,0:T(8,128)(2,1)S(1)}, bf16[48,2560]{1,0:T(8,128)(2,1)S(1)}, u32[]{:S(2)}, u32[]{:S(2)}) collective-permute-start(bf16[48,2560]{1,0:T(8,128)(2,1)S(1)} %get-tuple-element.56), channel_id=1, source_target_pairs={{0,8},{4,12},{8,16},{12,20},{16,24},{20,28},{24,0},{28,4},{1,9},{5... | collective-permute-start | bytes 737288 | tf_op jit(solution)/shard_map/ppermute | solution.py:431
  25.4 2.9 %collective-permute-start.5 = (bf16[48,2560]{1,0:T(8,128)(2,1)S(1)}, bf16[48,2560]{1,0:T(8,128)(2,1)S(1)}, u32[]{:S(2)}, u32[]{:S(2)}) collective-permute-start(bf16[48,2560]{1,0:T(8,128)(2,1)S(1)} %collective-permute-done.refs_2_), channel_id=1, source_target_pairs={{0,4},{4,0},{8,12},{12,8},{16,20},{20,16},{24,28},{28,24},{1,5},{5... | collective-permute-start | bytes 737288 | tf_op jit(solution)/shard_map/ppermute | solution.py:434
  25.4 10.5 %collective-permute-start.7 = (bf16[48,2560]{1,0:T(8,128)(2,1)S(1)}, bf16[48,2560]{1,0:T(8,128)(2,1)S(1)}, u32[]{:S(2)}, u32[]{:S(2)}) collective-permute-start(bf16[48,2560]{1,0:T(8,128)(2,1)S(1)} %collective-permute-done.1.refs_3_), channel_id=1, source_target_pairs={{0,8},{4,12},{8,16},{12,20},{16,24},{20,28},{24,0},{28,4},{1,9},{5... | collective-permute-start | bytes 737288 | tf_op jit(solution)/shard_map/ppermute | solution.py:431
  25.4 10.5 %collective-permute-start.6 = (bf16[48,2560]{1,0:T(8,128)(2,1)S(1)}, bf16[48,2560]{1,0:T(8,128)(2,1)S(1)}, u32[]{:S(2)}, u32[]{:S(2)}) collective-permute-start(bf16[48,2560]{1,0:T(8,128)(2,1)S(1)} %collective-permute-done.1.refs_3_), channel_id=1, source_target_pairs={{0,4},{4,0},{8,12},{12,8},{16,20},{20,16},{24,28},{28,24},{1,5},{5... | collective-permute-start | bytes 737288 | tf_op jit(solution)/shard_map/ppermute | solution.py:434
  26.6 14.2 %collective-permute-start.2 = (bf16[48,2560]{1,0:T(8,128)(2,1)S(1)}, bf16[48,2560]{1,0:T(8,128)(2,1)S(1)}, u32[]{:S(2)}, u32[]{:S(2)}) collective-permute-start(bf16[48,2560]{1,0:T(8,128)(2,1)S(1)} %collective-permute-done.refs_2_), channel_id=1, source_target_pairs={{0,8},{4,12},{8,16},{12,20},{16,24},{20,28},{24,0},{28,4},{1,9},{5... | collective-permute-start | bytes 737288 | tf_op jit(solution)/shard_map/ppermute | solution.py:431
  40.9 1.9 %collective-permute-start.8 = (bf16[48,2560]{1,0:T(8,128)(2,1)S(1)}, bf16[48,2560]{1,0:T(8,128)(2,1)S(1)}, u32[]{:S(2)}, u32[]{:S(2)}) collective-permute-start(bf16[48,2560]{1,0:T(8,128)(2,1)S(1)} %collective-permute-done.2.refs_6_), channel_id=1, source_target_pairs={{0,4},{4,0},{8,12},{12,8},{16,20},{20,16},{24,28},{28,24},{1,5},{5... | collective-permute-start | bytes 737288 | tf_op jit(solution)/shard_map/ppermute | solution.py:434
  40.9 10.7 %collective-permute-start.10 = (bf16[48,2560]{1,0:T(8,128)(2,1)S(1)}, bf16[48,2560]{1,0:T(8,128)(2,1)}, u32[]{:S(2)}, u32[]{:S(2)}) collective-permute-start(bf16[48,2560]{1,0:T(8,128)(2,1)S(1)} %collective-permute-done.7.refs_7_), channel_id=1, source_target_pairs={{0,8},{4,12},{8,16},{12,20},{16,24},{20,28},{24,0},{28,4},{1,9},{5... | collective-permute-start | bytes 737288 | tf_op jit(solution)/shard_map/ppermute | solution.py:431
  40.9 10.7 %collective-permute-start.9 = (bf16[48,2560]{1,0:T(8,128)(2,1)S(1)}, bf16[48,2560]{1,0:T(8,128)(2,1)S(1)}, u32[]{:S(2)}, u32[]{:S(2)}) collective-permute-start(bf16[48,2560]{1,0:T(8,128)(2,1)S(1)} %collective-permute-done.7.refs_7_), channel_id=1, source_target_pairs={{0,4},{4,0},{8,12},{12,8},{16,20},{20,16},{24,28},{28,24},{1,5},{5... | collective-permute-start | bytes 737288 | tf_op jit(solution)/shard_map/ppermute | solution.py:434
  42.1 14.3 %collective-permute-start.3 = (bf16[48,2560]{1,0:T(8,128)(2,1)S(1)}, bf16[48,2560]{1,0:T(8,128)(2,1)}, u32[]{:S(2)}, u32[]{:S(2)}) collective-permute-start(bf16[48,2560]{1,0:T(8,128)(2,1)S(1)} %collective-permute-done.2.refs_6_), channel_id=1, source_target_pairs={{0,8},{4,12},{8,16},{12,20},{16,24},{20,28},{24,0},{28,4},{1,9},{5... | collective-permute-start | bytes 737288 | tf_op jit(solution)/shard_map/ppermute | solution.py:431
  42.8 18.1 %collective-permute-start.4 = (bf16[96,2560]{1,0:T(8,128)(2,1)S(1)}, bf16[96,2560]{1,0:T(8,128)(2,1)}, u32[]{:S(2)}, u32[]{:S(2)}) collective-permute-start(bf16[96,2560]{1,0:T(8,128)(2,1)S(1)} %bitcast.25), channel_id=1, source_target_pairs={{0,4},{4,0},{8,12},{12,8},{16,20},{20,16},{24,28},{28,24},{1,5},{5... | collective-permute-start | bytes 1474568 | tf_op jit(solution)/shard_map/ppermute | solution.py:434
  52.2 7.8 %collective-permute-start.12 = (bf16[48,2560]{1,0:T(8,128)(2,1)}, bf16[48,2560]{1,0:T(8,128)(2,1)}, u32[]{:S(2)}, u32[]{:S(2)}) collective-permute-start(bf16[48,2560]{1,0:T(8,128)(2,1)} %collective-permute-done.10.refs_11_), channel_id=1, source_target_pairs={{0,4},{4,0},{8,12},{12,8},{16,20},{20,16},{24,28},{28,24},{1,5},{5... | collective-permute-start | bytes 737288 | tf_op jit(solution)/shard_map/ppermute | solution.py:434
  56.4 4.5 %collective-permute-start.11 = (bf16[48,2560]{1,0:T(8,128)(2,1)}, bf16[48,2560]{1,0:T(8,128)(2,1)}, u32[]{:S(2)}, u32[]{:S(2)}) collective-permute-start(bf16[48,2560]{1,0:T(8,128)(2,1)} %collective-permute-done.3.refs_10_), channel_id=1, source_target_pairs={{0,4},{4,0},{8,12},{12,8},{16,20},{20,16},{24,28},{28,24},{1,5},{5... | collective-permute-start | bytes 737288 | tf_op jit(solution)/shard_map/ppermute | solution.py:434
  56.4 41.3 %all-to-all-start = ((bf16[8,128,384]{2,1,0:T(8,128)(2,1)}), bf16[8,128,384]{2,1,0:T(8,128)(2,1)S(1)}, u32[]{:S(2)}, u32[]{:S(2)}) async-start(bf16[8,128,384]{2,1,0:T(8,128)(2,1)} %window.1), calls=%async_computation | async-start | bytes 1572864 | tf_op jit(solution)/shard_map/all_to_all | solution.py:437
  68.2 26.5 %collective-permute-start.13 = (bf16[256,1536]{1,0:T(8,128)(2,1)}, bf16[256,1536]{1,0:T(8,128)(2,1)}, u32[]{:S(2)}, u32[]{:S(2)}) collective-permute-start(bf16[256,1536]{1,0:T(8,128)(2,1)} %get-tuple-element.44.refs_0_), channel_id=1, source_target_pairs={{0,8},{4,12},{8,16},{12,20},{16,24},{20,28},{24,0},{28,4},{1,9},{5... | collective-permute-start | bytes 2359304 | tf_op jit(solution)/shard_map/ppermute | solution.py:431
  94.6 21.1 %collective-permute-start.14 = (bf16[256,1536]{1,0:T(8,128)(2,1)}, bf16[256,1536]{1,0:T(8,128)(2,1)}, u32[]{:S(2)}, u32[]{:S(2)}) collective-permute-start(bf16[256,1536]{1,0:T(8,128)(2,1)} %collective-permute-done.13.refs_2_), channel_id=1, source_target_pairs={{0,8},{4,12},{8,16},{12,20},{16,24},{20,28},{24,0},{28,4},{1,9},{5... | collective-permute-start | bytes 2359304 | tf_op jit(solution)/shard_map/ppermute | solution.py:431
  99.5 22.9 %all-to-all-start.2 = ((bf16[4,8,64,384]{3,2,1,0:T(8,128)(2,1)}), bf16[4,8,64,384]{3,2,1,0:T(8,128)(2,1)S(1)}, u32[]{:S(2)}, u32[]{:S(2)}) async-start(bf16[4,8,64,384]{3,2,1,0:T(8,128)(2,1)} %compact.1), calls=%async_computation.2 | async-start | bytes 3145728 | tf_op jit(solution)/shard_map/all_to_all | solution.py:437
  103.4 20.2 %collective-permute-start.17 = (bf16[256,1536]{1,0:T(8,128)(2,1)}, bf16[256,1536]{1,0:T(8,128)(2,1)}, u32[]{:S(2)}, u32[]{:S(2)}) collective-permute-start(bf16[256,1536]{1,0:T(8,128)(2,1)} %get-tuple-element.44.refs_0_), channel_id=1, source_target_pairs={{0,4},{4,0},{8,12},{12,8},{16,20},{20,16},{24,28},{28,24},{1,5},{5... | collective-permute-start | bytes 2359304 | tf_op jit(solution)/shard_map/ppermute | solution.py:434
  103.4 20.2 %collective-permute-start.18 = (bf16[256,1536]{1,0:T(8,128)(2,1)}, bf16[256,1536]{1,0:T(8,128)(2,1)}, u32[]{:S(2)}, u32[]{:S(2)}) collective-permute-start(bf16[256,1536]{1,0:T(8,128)(2,1)} %collective-permute-done.13.refs_2_), channel_id=1, source_target_pairs={{0,4},{4,0},{8,12},{12,8},{16,20},{20,16},{24,28},{28,24},{1,5},{5... | collective-permute-start | bytes 2359304 | tf_op jit(solution)/shard_map/ppermute | solution.py:434
  115.8 11.0 %collective-permute-start.16 = (bf16[256,1536]{1,0:T(8,128)(2,1)}, bf16[256,1536]{1,0:T(8,128)(2,1)S(1)}, u32[]{:S(2)}, u32[]{:S(2)}) collective-permute-start(bf16[256,1536]{1,0:T(8,128)(2,1)} %collective-permute-done.14.refs_0_), channel_id=1, source_target_pairs={{0,4},{4,0},{8,12},{12,8},{16,20},{20,16},{24,28},{28,24},{1,5},{5... | collective-permute-start | bytes 2359304 | tf_op jit(solution)/shard_map/ppermute | solution.py:434
  115.8 22.1 %collective-permute-start.15 = (bf16[256,1536]{1,0:T(8,128)(2,1)}, bf16[256,1536]{1,0:T(8,128)(2,1)S(1)}, u32[]{:S(2)}, u32[]{:S(2)}) collective-permute-start(bf16[256,1536]{1,0:T(8,128)(2,1)} %collective-permute-done.14.refs_0_), channel_id=1, source_target_pairs={{0,8},{4,12},{8,16},{12,20},{16,24},{20,28},{24,0},{28,4},{1,9},{5... | collective-permute-start | bytes 2359304 | tf_op jit(solution)/shard_map/ppermute | solution.py:431
  117.7 11.1 %collective-permute-start.19 = (f32[3,120,128]{2,1,0:T(8,128)}, f32[3,120,128]{2,1,0:T(8,128)S(1)}, u32[]{:S(2)}, u32[]{:S(2)}) collective-permute-start(f32[3,120,128]{2,1,0:T(8,128)} %heads.1), channel_id=1, source_target_pairs={{4,0},{8,4},{12,8},{16,12},{20,16},{24,20},{28,24},{5,1},{9,5},{13... | collective-permute-start | bytes 552968 | tf_op jit(solution)/shard_map/ppermute | solution.py:544
  137.9 3.6 %collective-permute-start.20 = (bf16[256,1536]{1,0:T(8,128)(2,1)S(1)}, bf16[256,1536]{1,0:T(8,128)(2,1)S(1)}, u32[]{:S(2)}, u32[]{:S(2)}) collective-permute-start(bf16[256,1536]{1,0:T(8,128)(2,1)S(1)} %collective-permute-done.15.own_ref), channel_id=1, source_target_pairs={{0,4},{4,0},{8,12},{12,8},{16,20},{20,16},{24,28},{28,24},{1,5},{5... | collective-permute-start | bytes 2359304 | tf_op jit(solution)/shard_map/ppermute | solution.py:434
  (24 other events, 102.5 us)

commit v2 on v0

--- a/solution.py
+++ b/solution.py
@@ -38,9 +38,8 @@
     return pl.CostEstimate(flops=int(flops), bytes_accessed=int(moved), transcendentals=0)
 
 
-def pack_kernel(
-    routes_ref, weight_ref, grads_any, saved_any, select_ref, target_ref, packed_any, grads, saved, packed, sems
-):
+def pack_kernel(me_ref, routes_ref, weight_ref, grads_any, saved_any, select_ref, target_ref, *refs):
+    packed_anys, (grads, saved, packed, sems) = refs[:-4], refs[-4:]
     loads = [
         pltpu.make_async_copy(grads_any, grads, sems.at[0]),
         pltpu.make_async_copy(saved_any, saved, sems.at[1]),
@@ -72,7 +71,8 @@
         packed[k, :, :width] = picked_grads[span]
         packed[k, :, width:-LANES] = picked_saved[span]
         packed[k, :, -LANES:] = weight[span]
-        stores.append(pltpu.make_async_copy(packed.at[k], packed_any.at[k], sems.at[2 + k]))
+    for k, packed_any in enumerate(packed_anys):
+        stores.append(pltpu.make_async_copy(packed.at[me_ref[0] ^ k], packed_any, sems.at[2 + k]))
         stores[-1].start()
     for store in stores:
         store.wait()
@@ -126,21 +126,25 @@
         out_ref[i] = slab.T[width - kept :, :]
 
 
-def factor_kernel(arrived_ref, grads_ref, gate_ref, up_ref, score_ref):
+def factor_kernel(me_ref, *refs):
+    arrived_refs, (grads_ref, gate_ref, up_ref, score_ref) = refs[:-4], refs[-4:]
     width, hidden = grads_ref.shape[1], gate_ref.shape[1]
-    grads_ref[...] = arrived_ref[:, :width]
-    gate = arrived_ref[:, width : width + hidden].astype(f32)
-    up = arrived_ref[:, width + hidden : width + 2 * hidden].astype(f32)
-    weight = arrived_ref[:, width + 2 * hidden :].astype(f32)[:, 0:1]
-    sig = jax.nn.sigmoid(gate)
-    act = gate * sig
-    score_ref[...] = act * up
-    up_ref[...] = weight * act
-    gate_ref[...] = weight * (up * sig * (1.0 + gate * (1.0 - sig)))
+    cap = arrived_refs[0].shape[0]
+    for k, arrived_ref in enumerate(arrived_refs):
+        span = pl.ds(pl.multiple_of((me_ref[0] ^ k) * cap, 16), cap)
+        grads_ref[span, :] = arrived_ref[:, :width]
+        gate = arrived_ref[:, width : width + hidden].astype(f32)
+        up = arrived_ref[:, width + hidden : width + 2 * hidden].astype(f32)
+        weight = arrived_ref[:, width + 2 * hidden :].astype(f32)[:, 0:1]
+        sig = jax.nn.sigmoid(gate)
+        act = gate * sig
+        score_ref[span, :] = act * up
+        up_ref[span, :] = weight * act
+        gate_ref[span, :] = weight * (up * sig * (1.0 + gate * (1.0 - sig)))
 
 
 def row_kernel(position_ref, grads_ref, gate_factor, up_factor, score_factor, *refs, chips):
-    down_refs, refs = refs[:-6], refs[-5:]
+    down_refs, refs = refs[:-5], refs[-5:]
     joined_any, scores_ref, joined, down, sems = refs
     hidden = down.shape[0]
     loads = []
@@ -188,10 +192,6 @@
 def head_kernel(master_ref, first_ref, second_ref, out_ref):
     for n, source in enumerate((master_ref, first_ref, second_ref)):
         out_ref[n] = source[...]
-
-
-def ready_kernel(*refs):
-    refs[-1][...] = jnp.zeros(refs[-1].shape, f32)
 
 
 def slab_sum(total, turned_ref, slabs, joined_refs, span):
@@ -439,25 +439,27 @@
         return lax.optimization_barrier(values)
 
     wide = model_width + columns + LANES
-    select, target, packed = pl.pallas_call(
+    me = lax.axis_index("expert").astype(i32).reshape(1)
+    select, target, *packed = pl.pallas_call(
         pack_kernel,
         out_shape=[
             struct((rows, token_count), f32),
             struct((1, token_count), f32),
-            struct((experts, cap, wide), bf16),
-        ],
-        in_specs=[vmem(), vmem(), hbm(), hbm()],
-        out_specs=[vmem(), vmem(), hbm()],
+        ]
+        + [struct((cap, wide), bf16)] * experts,
+        in_specs=[smem(), vmem(), vmem(), hbm(), hbm()],
+        out_specs=[vmem(), vmem()] + [hbm()] * experts,
         scratch_shapes=[
             pltpu.VMEM((token_count, model_width), bf16),
             pltpu.VMEM((token_count, columns), bf16),
             pltpu.VMEM((experts, cap, wide), bf16),
             pltpu.SemaphoreType.DMA((2 + experts,)),
         ],
-        compiler_params=params(16),
+        compiler_params=params(60),
         cost_estimate=cost(0, 6_000_000),
         name="pack",
     )(
+        me,
         routes.reshape(1, token_count),
         route_weight.reshape(1, token_count),
         out_grad,
@@ -472,46 +474,37 @@
         12,
         moved=2_000_000,
     )
+    arrived = packed[:1] + [
+        lax.ppermute(packed[k], "expert", [(i, i ^ k) for i in range(experts)]) for k in range(1, experts)
+    ]
+    windows = exchanged(windows, "dp")
     if down_weight.shape[1] % 16 == 0:
         held, other = [down_weight[0]], [swapped(down_weight[0])]
         for k in range(1, chips):
             arrival = onward(held[-1])
-            if k == 1:
-                arrival, windows = tied(arrival, windows)
-            else:
-                arrival, other = tied(arrival, other)
             held.append(arrival)
-            other.append(swapped(arrival))
-            if k == chips - 1:
-                windows, held[-1] = tied(windows, held[-1])
+            if k == chips - 2:
+                held[-1], arrived[1], arrived[2] = tied(held[-1], arrived[1], arrived[2])
+                arrived[-1], windows, block = tied(arrived[-1], windows, held[-1])
+                other.append(swapped(block))
+                continue
+            other.append(swapped(held[-1]))
         down = [piece for pair in zip(held, other) for piece in pair]
     else:
         down = [lax.all_gather(down_weight, "dp", axis=1, tiled=True)[0]]
-        windows, down[0] = tied(windows, down[0])
-    arrived = exchanged(packed, "expert").reshape(rows, wide)
-    windows = exchanged(windows, "dp")
     factors = call(
         factor_kernel,
         [struct((rows, model_width), bf16)] + [struct((rows, hidden), f32)] * 3,
-        (),
-        (arrived,),
+        (me,),
+        arrived,
         "factors",
         20,
         moved=6_000_000,
     )
-    ready = pl.pallas_call(
-        ready_kernel,
-        out_shape=struct((8, LANES), f32),
-        in_specs=[anywhere()],
-        out_specs=vmem(),
-        compiler_params=params(4),
-        cost_estimate=cost(0, 18_000_000),
-        name="ready",
-    )(down[-1])
     joined, scores = pl.pallas_call(
         functools.partial(row_kernel, chips=chips),
         out_shape=[struct((rows, columns), bf16), struct((rows, LANES), f32)],
-        in_specs=[smem()] + [vmem()] * 4 + [anywhere()] * (len(down) + 1),
+        in_specs=[smem()] + [vmem()] * 4 + [anywhere()] * len(down),
         out_specs=[hbm(), vmem()],
         scratch_shapes=[
             pltpu.VMEM((rows, columns), bf16),
@@ -521,7 +514,7 @@
         compiler_params=params(24),
         cost_estimate=cost(2 * rows * model_width * hidden, 8_000_000),
         name="rows",
-    )(position, *factors, *down, ready)
+    )(position, *factors, *down)
 
     steps = [[joined, swapped(joined)]]
     step_one = onward(joined)

time: 140 us -> 139 us (level)
  local copies, waits for them, and re-layouts: 9.32 us -> 1.77 us
  waiting for transfers between devices: 82.8 us -> 87.5 us
  Pallas kernels: 23.8 us -> 26.2 us
    ppermute x0 -> x3, waiting for transfers between devices: none -> 22.2 us  [shards(): lax.ppermute(packed[k], 'expert', [(i, i ^ k) for i in range(experts)])]
    ppermute x6, waiting for transfers between devices: 74.6 us -> 60.6 us  [onward(): lax.ppermute(block, 'dp', [(i, (i + 2) % parts) for i in range(parts)])]
    unnamed x44 -> x18, local copies, waits for them, and re-layouts: 9.32 us -> 1.77 us
    all_to_all x3 -> x2, starting transfers between devices: 11.1 us -> 7.58 us  [exchanged(): return lax.all_to_all(block, axis, split_axis=0, concat_axis=0, tiled=True)]
    ppermute x0 -> x3, starting transfers between devices: none -> 3.49 us  [shards(): lax.ppermute(packed[k], 'expert', [(i, i ^ k) for i in range(experts)])]
    all_to_all x3 -> x2, waiting for transfers between devices: 4.68 us -> 1.47 us  [exchanged(): return lax.all_to_all(block, axis, split_axis=0, concat_axis=0, tiled=True)]
    pallas_call x1, Pallas kernels: 1.8 us -> 4.66 us  [shards(): pl.pallas_call(pack_kernel, out_shape=[struct((rows, token_count), f32),...]
  transfers between devices with their start and end apart: 18 -> 20, of which waited for: 11 -> 11; matrix products, arithmetic and copies ran while one was open for 0% -> 0% of each run, Pallas kernels for 13% -> 12%
where the time goes in v2:
time: 139 us
  waiting for transfers between devices  87.5 us (63%)
  Pallas kernels  26.2 us (19%)
  starting transfers between devices  22.4 us (16%)
  local copies, waits for them, and re-layouts  1.77 us (1%)
    ppermute x6, waiting for transfers between devices, onward(): lax.ppermute(block, 'dp', [(i, (i + 2) % parts) for i in range(parts)])  60.6 us
    ppermute x3, waiting for transfers between devices, shards(): lax.ppermute(packed[k], 'expert', [(i, i ^ k) for i in range(experts)])  22.2 us
    pallas_call x7, Pallas kernels, call(): pl.pallas_call(kernel, out_shape=outs, in_specs=[smem()] * len(scalars) +...  9.95 us
    all_to_all x2, starting transfers between devices, exchanged(): return lax.all_to_all(block, axis, split_axis=0, concat_axis=0, tiled=True)  7.58 us
    ppermute x6, starting transfers between devices, onward(): lax.ppermute(block, 'dp', [(i, (i + 2) % parts) for i in range(parts)])  7.18 us
    pallas_call x1, Pallas kernels, shards(): pl.pallas_call(functools.partial(final_kernel, even_size=even_size, head_...  5.7 us
    pallas_call x1, Pallas kernels, shards(): pl.pallas_call(pack_kernel, out_shape=[struct((rows, token_count), f32),...  4.66 us
    pallas_call x1, Pallas kernels, shards(): pl.pallas_call(functools.partial(row_kernel, chips=chips), out_shape=[str...  4.36 us
  transfers between devices with their start and end apart: 20, of which 11 were waited for; matrix products, arithmetic and copies ran while one was open for 0% of the time, Pallas kernels for 12%

profile of v2, /device:TPU:0, one launch (start us, length us, event | category | flops | bytes accessed | tf_op | source)
XLA Modules:
  0.0 138.7 jit_solution(14962318968838186411)
XLA Ops:
  0.6 3.1 %collective-permute-start.1 = (bf16[96,2560]{1,0:T(8,128)(2,1)}, bf16[96,2560]{1,0:T(8,128)(2,1)}, u32[]{:S(2)}, u32[]{:S(2)}) collective-permute-start(bf16[96,2560]{1,0:T(8,128)(2,1)} %bitcast.20), channel_id=1, source_target_pairs={{0,8},{4,12},{8,16},{12,20},{16,24},{20,28},{24,0},{28,4},{1,9},{5... | collective-permute-start | bytes 1474568 | tf_op jit(solution)/shard_map/ppermute | solution.py:430
  3.7 4.7 %pack.1 = (f32[256,128]{1,0:T(8,128)}, f32[1,128]{1,0:T(1,128)}, bf16[64,4224]{1,0:T(8,128)(2,1)}, bf16[64,4224]{1,0:T(8,128)(2,1)}, bf16[64,4224]{1,0:T(8,128)(2,1)}, /*index=5*/bf16[64,4224]{1,0:T(8,128)(2,1)}) custom-call(s32[1]{0:T(128)} %bitcast.1.me_ref, s32[1,128]{1,0:T(1,128)} %bitcast.24, bf16[1,128]{1,0:T(2,128)(2,1)} %bitcast.25, ...), custom_call_target="tpu_custom_call" | custom-call | bytes 6000000 | tf_op jit(solution)/shard_map/pack/pallas_call | solution.py:443
  11.2 3.9 %all-to-all-start = ((bf16[8,128,384]{2,1,0:T(8,128)(2,1)}), bf16[8,128,384]{2,1,0:T(8,128)(2,1)S(1)}, u32[]{:S(2)}, u32[]{:S(2)}) async-start(bf16[8,128,384]{2,1,0:T(8,128)(2,1)} %window.1), calls=%async_computation | async-start | bytes 1572864 | tf_op jit(solution)/shard_map/all_to_all | solution.py:436
  15.1 1.5 %collective-permute-start.3 = (bf16[64,4224]{1,0:T(8,128)(2,1)}, bf16[64,4224]{1,0:T(8,128)(2,1)S(1)}, u32[]{:S(2)}, u32[]{:S(2)}) collective-permute-start(bf16[64,4224]{1,0:T(8,128)(2,1)} %get-tuple-element.34), channel_id=1, source_target_pairs={{0,1},{1,0},{2,3},{3,2},{4,5},{5,4},{6,7},{7,6},{8,9},{9,8},{10,11... | collective-permute-start | bytes 1622024 | tf_op jit(solution)/shard_map/ppermute | solution.py:478
  16.6 1.5 %collective-permute-start.4 = (bf16[64,4224]{1,0:T(8,128)(2,1)}, bf16[64,4224]{1,0:T(8,128)(2,1)S(1)}, u32[]{:S(2)}, u32[]{:S(2)}) collective-permute-start(bf16[64,4224]{1,0:T(8,128)(2,1)} %get-tuple-element.35), channel_id=1, source_target_pairs={{0,2},{1,3},{2,0},{3,1},{4,6},{5,7},{6,4},{7,5},{8,10},{9,11},{10,... | collective-permute-start | bytes 1622024 | tf_op jit(solution)/shard_map/ppermute | solution.py:478
  18.1 2.0 %collective-permute-start.2 = (bf16[96,2560]{1,0:T(8,128)(2,1)}, bf16[96,2560]{1,0:T(8,128)(2,1)}, u32[]{:S(2)}, u32[]{:S(2)}) collective-permute-start(bf16[96,2560]{1,0:T(8,128)(2,1)} %collective-permute-done.1.refs_2_), channel_id=1, source_target_pairs={{0,8},{4,12},{8,16},{12,20},{16,24},{20,28},{24,0},{28,4},{1,9},{5... | collective-permute-start | bytes 1474568 | tf_op jit(solution)/shard_map/ppermute | solution.py:430
  20.6 9.8 %collective-permute-done.3.refs_1_ = bf16[64,4224]{1,0:T(8,128)(2,1)S(1)} collective-permute-done((bf16[64,4224]{1,0:T(8,128)(2,1)}, bf16[64,4224]{1,0:T(8,128)(2,1)S(1)}, u32[]{:S(2)}, u32[]{:S(2)}) %collective-permute-start.3) | collective-permute-done | bytes 540704 | tf_op jit(solution)/shard_map/ppermute | solution.py:478
  30.4 12.4 %collective-permute-done.4.refs_2_ = bf16[64,4224]{1,0:T(8,128)(2,1)S(1)} collective-permute-done((bf16[64,4224]{1,0:T(8,128)(2,1)}, bf16[64,4224]{1,0:T(8,128)(2,1)S(1)}, u32[]{:S(2)}, u32[]{:S(2)}) %collective-permute-start.4) | collective-permute-done | bytes 540704 | tf_op jit(solution)/shard_map/ppermute | solution.py:478
  43.5 1.7 %collective-permute-start.8 = (bf16[96,2560]{1,0:T(8,128)(2,1)}, bf16[96,2560]{1,0:T(8,128)(2,1)}, u32[]{:S(2)}, u32[]{:S(2)}) collective-permute-start(bf16[96,2560]{1,0:T(8,128)(2,1)} %collective-permute-done.2.refs_4_), channel_id=1, source_target_pairs={{0,8},{4,12},{8,16},{12,20},{16,24},{20,28},{24,0},{28,4},{1,9},{5... | collective-permute-start | bytes 1474568 | tf_op jit(solution)/shard_map/ppermute | solution.py:430
  46.6 11.7 %collective-permute-done.8.refs_6_ = bf16[96,2560]{1,0:T(8,128)(2,1)} collective-permute-done((bf16[96,2560]{1,0:T(8,128)(2,1)}, bf16[96,2560]{1,0:T(8,128)(2,1)}, u32[]{:S(2)}, u32[]{:S(2)}) %collective-permute-start.8) | collective-permute-done | bytes 491552 | tf_op jit(solution)/shard_map/ppermute | solution.py:430
  59.2 1.4 %collective-permute-done.9.refs_7_ = bf16[96,2560]{1,0:T(8,128)(2,1)} collective-permute-done((bf16[96,2560]{1,0:T(8,128)(2,1)}, bf16[96,2560]{1,0:T(8,128)(2,1)}, u32[]{:S(2)}, u32[]{:S(2)}) %collective-permute-start.9) | collective-permute-done | bytes 491552 | tf_op jit(solution)/shard_map/ppermute | solution.py:433
  60.6 4.4 %rows.1 = (bf16[256,1536]{1,0:T(8,128)(2,1)}, f32[256,128]{1,0:T(8,128)S(1)}) custom-call(s32[1]{0:T(128)} %bitcast.position_ref, bf16[256,2560]{1,0:T(8,128)(2,1)S(1)} %get-tuple-element.42.grads_ref, f32[256,768]{1,0:T(8,128)S(1)} %get-tuple-element.43.gate_factor, f32[256,768]{1,0:T(8,128)S(1)} %get-tuple-element.44.up_factor, ...), custom_call_target="tpu_custom_call" | custom-call | flops 1006632960 | bytes 8000000 | tf_op jit(solution)/shard_map/rows/pallas_call | solution.py:504
  65.3 21.3 %collective-permute-done.10.refs_2_ = bf16[256,1536]{1,0:T(8,128)(2,1)} collective-permute-done((bf16[256,1536]{1,0:T(8,128)(2,1)}, bf16[256,1536]{1,0:T(8,128)(2,1)}, u32[]{:S(2)}, u32[]{:S(2)}) %collective-permute-start.10) | collective-permute-done | bytes 786464 | tf_op jit(solution)/shard_map/ppermute | solution.py:430
  86.7 1.8 %compact.1 = bf16[4,8,64,384]{3,2,1,0:T(8,128)(2,1)} custom-call(s32[1]{0:T(128)} %bitcast.position_ref, bf16[8,128,384]{2,1,0:T(8,128)(2,1)S(1)} %all-to-all-done.windows_ref, f32[256,128]{1,0:T(8,128)S(1)} %get-tuple-element.47.scores_ref), custom_call_target="tpu_custom_call" | custom-call | bytes 3000000 | tf_op jit(solution)/shard_map/compact/pallas_call | solution.py:378
  88.5 3.7 %all-to-all-start.1 = ((bf16[4,8,64,384]{3,2,1,0:T(8,128)(2,1)}), bf16[4,8,64,384]{3,2,1,0:T(8,128)(2,1)S(1)}, u32[]{:S(2)}, u32[]{:S(2)}) async-start(bf16[4,8,64,384]{3,2,1,0:T(8,128)(2,1)} %compact.1), calls=%async_computation.1 | async-start | bytes 3145728 | tf_op jit(solution)/shard_map/all_to_all | solution.py:436
  92.7 14.7 %collective-permute-done.11.refs_0_ = bf16[256,1536]{1,0:T(8,128)(2,1)S(1)} collective-permute-done((bf16[256,1536]{1,0:T(8,128)(2,1)}, bf16[256,1536]{1,0:T(8,128)(2,1)S(1)}, u32[]{:S(2)}, u32[]{:S(2)}) %collective-permute-start.11) | collective-permute-done | bytes 786464 | tf_op jit(solution)/shard_map/ppermute | solution.py:430
  107.5 1.6 %heads.1 = f32[3,120,128]{2,1,0:T(8,128)} custom-call(f32[3960,128]{1,0:T(8,128)} %bitcast.14, f32[3960,128]{1,0:T(8,128)} %bitcast.16, f32[3960,128]{1,0:T(8,128)} %bitcast.18), custom_call_target="tpu_custom_call" | custom-call | bytes 400000 | tf_op jit(solution)/shard_map/heads/pallas_call | solution.py:521
  109.0 1.4 %collective-permute-start.16 = (f32[3,120,128]{2,1,0:T(8,128)}, f32[3,120,128]{2,1,0:T(8,128)S(1)}, u32[]{:S(2)}, u32[]{:S(2)}) collective-permute-start(f32[3,120,128]{2,1,0:T(8,128)} %heads.1), channel_id=1, source_target_pairs={{4,0},{8,4},{12,8},{16,12},{20,16},{24,20},{28,24},{5,1},{9,5},{13... | collective-permute-start | bytes 552968 | tf_op jit(solution)/shard_map/ppermute | solution.py:531
  112.2 3.1 %early1.1.refs_2_ = f32[336,1536]{1,0:T(8,128)S(1)} custom-call(s32[1]{0:T(128)} %bitcast.position_ref, bf16[8,336,256]{2,1,0:T(8,128)(2,1)S(1)} %turn.1.turned_ref, bf16[256,1536]{1,0:T(8,128)(2,1)} %get-tuple-element.48.refs_0_, bf16[256,1536]{1,0:T(8,128)(2,1)} %collective-permute-done.14.refs_1_, bf16[256,1536]{1,0:T(8,128)(2,1)} %collective-permute-done.10.refs_2_, ...), custom_call_target="tpu_custom_call" | custom-call | flops 1056964608 | bytes 8000000 | tf_op jit(solution)/shard_map/early1/pallas_call | solution.py:378
  115.4 2.0 %early2.1.early_ref = f32[336,1536]{1,0:T(8,128)S(1)} custom-call(s32[1]{0:T(128)} %bitcast.position_ref, bf16[8,336,256]{2,1,0:T(8,128)(2,1)S(1)} %turn.1.turned_ref, bf16[256,1536]{1,0:T(8,128)(2,1)S(1)} %collective-permute-done.11.refs_0_, bf16[256,1536]{1,0:T(8,128)(2,1)} %collective-permute-done.13.refs_1_, f32[336,1536]{1,0:T(8,128)S(1)} %early1.1.refs_2_), custom_call_target="tpu_custom_call" | custom-call | flops 528482304 | bytes 8000000 | tf_op jit(solution)/shard_map/early2/pallas_call | solution.py:378
  117.4 12.0 %collective-permute-done.12.own_ref = bf16[256,1536]{1,0:T(8,128)(2,1)S(1)} collective-permute-done((bf16[256,1536]{1,0:T(8,128)(2,1)S(1)}, bf16[256,1536]{1,0:T(8,128)(2,1)S(1)}, u32[]{:S(2)}, u32[]{:S(2)}) %collective-permute-start.12) | collective-permute-done | bytes 786464 | tf_op jit(solution)/shard_map/ppermute | solution.py:430
  129.4 1.7 %collective-permute-start.17 = (bf16[256,1536]{1,0:T(8,128)(2,1)S(1)}, bf16[256,1536]{1,0:T(8,128)(2,1)S(1)}, u32[]{:S(2)}, u32[]{:S(2)}) collective-permute-start(bf16[256,1536]{1,0:T(8,128)(2,1)S(1)} %collective-permute-done.12.own_ref), channel_id=1, source_target_pairs={{0,4},{4,0},{8,12},{12,8},{16,20},{20,16},{24,28},{28,24},{1,5},{5... | collective-permute-start | bytes 2359304 | tf_op jit(solution)/shard_map/ppermute | solution.py:433
  131.1 1.9 %collective-permute-done.17.other_ref = bf16[256,1536]{1,0:T(8,128)(2,1)S(1)} collective-permute-done((bf16[256,1536]{1,0:T(8,128)(2,1)S(1)}, bf16[256,1536]{1,0:T(8,128)(2,1)S(1)}, u32[]{:S(2)}, u32[]{:S(2)}) %collective-permute-start.17) | collective-permute-done | bytes 786464 | tf_op jit(solution)/shard_map/ppermute | solution.py:433
  133.0 5.7 %final.1 = (f32[3960,128]{1,0:T(8,128)}, f32[3960,128]{1,0:T(8,128)}, f32[3960,128]{1,0:T(8,128)}, bf16[320,1536]{1,0:T(8,128)(2,1)}) custom-call(s32[1]{0:T(128)} %bitcast.position_ref, s32[9]{0:T(128)S(1)} %copy-done.7, bf16[8,336,256]{2,1,0:T(8,128)(2,1)S(1)} %turn.1.turned_ref, f32[336,1536]{1,0:T(8,128)S(1)} %early2.1.early_ref, ...), custom_call_target="tpu_custom_call" | custom-call | flops 528482304 | bytes 25000000 | tf_op jit(solution)/shard_map/final/pallas_call | solution.py:590
  (45 shorter events, 9.0 us)
Async XLA Ops:
  0.6 17.5 %collective-permute-start.1 = (bf16[96,2560]{1,0:T(8,128)(2,1)}, bf16[96,2560]{1,0:T(8,128)(2,1)}, u32[]{:S(2)}, u32[]{:S(2)}) collective-permute-start(bf16[96,2560]{1,0:T(8,128)(2,1)} %bitcast.20), channel_id=1, source_target_pairs={{0,8},{4,12},{8,16},{12,20},{16,24},{20,28},{24,0},{28,4},{1,9},{5... | collective-permute-start | bytes 1474568 | tf_op jit(solution)/shard_map/ppermute | solution.py:430
  3.7 41.5 %copy-start.5 = (bf16[1,96,2560]{2,1,0:T(8,128)(2,1)S(1)}, bf16[1,96,2560]{2,1,0:T(8,128)(2,1)}, u32[]{:S(2)}) copy-start(bf16[1,96,2560]{2,1,0:T(8,128)(2,1)} %param.15) | copy-start | bytes 1474564
  10.1 48.2 %copy-start.4 = (bf16[64,4224]{1,0:T(8,128)(2,1)S(1)}, bf16[64,4224]{1,0:T(8,128)(2,1)}, u32[]{:S(2)}) copy-start(bf16[64,4224]{1,0:T(8,128)(2,1)} %get-tuple-element.38.refs_0_) | copy-start | bytes 1622020
  11.2 35.4 %all-to-all-start = ((bf16[8,128,384]{2,1,0:T(8,128)(2,1)}), bf16[8,128,384]{2,1,0:T(8,128)(2,1)S(1)}, u32[]{:S(2)}, u32[]{:S(2)}) async-start(bf16[8,128,384]{2,1,0:T(8,128)(2,1)} %window.1), calls=%async_computation | async-start | bytes 1572864 | tf_op jit(solution)/shard_map/all_to_all | solution.py:436
  15.1 15.3 %collective-permute-start.3 = (bf16[64,4224]{1,0:T(8,128)(2,1)}, bf16[64,4224]{1,0:T(8,128)(2,1)S(1)}, u32[]{:S(2)}, u32[]{:S(2)}) collective-permute-start(bf16[64,4224]{1,0:T(8,128)(2,1)} %get-tuple-element.34), channel_id=1, source_target_pairs={{0,1},{1,0},{2,3},{3,2},{4,5},{5,4},{6,7},{7,6},{8,9},{9,8},{10,11... | collective-permute-start | bytes 1622024 | tf_op jit(solution)/shard_map/ppermute | solution.py:478
  16.6 26.2 %collective-permute-start.4 = (bf16[64,4224]{1,0:T(8,128)(2,1)}, bf16[64,4224]{1,0:T(8,128)(2,1)S(1)}, u32[]{:S(2)}, u32[]{:S(2)}) collective-permute-start(bf16[64,4224]{1,0:T(8,128)(2,1)} %get-tuple-element.35), channel_id=1, source_target_pairs={{0,2},{1,3},{2,0},{3,1},{4,6},{5,7},{6,4},{7,5},{8,10},{9,11},{10,... | collective-permute-start | bytes 1622024 | tf_op jit(solution)/shard_map/ppermute | solution.py:478
  18.1 25.4 %collective-permute-start.2 = (bf16[96,2560]{1,0:T(8,128)(2,1)}, bf16[96,2560]{1,0:T(8,128)(2,1)}, u32[]{:S(2)}, u32[]{:S(2)}) collective-permute-start(bf16[96,2560]{1,0:T(8,128)(2,1)} %collective-permute-done.1.refs_2_), channel_id=1, source_target_pairs={{0,8},{4,12},{8,16},{12,20},{16,24},{20,28},{24,0},{28,4},{1,9},{5... | collective-permute-start | bytes 1474568 | tf_op jit(solution)/shard_map/ppermute | solution.py:430
  20.1 25.6 %collective-permute-start = (bf16[64,4224]{1,0:T(8,128)(2,1)}, bf16[64,4224]{1,0:T(8,128)(2,1)S(1)}, u32[]{:S(2)}, u32[]{:S(2)}) collective-permute-start(bf16[64,4224]{1,0:T(8,128)(2,1)} %get-tuple-element.32), channel_id=1, source_target_pairs={{0,3},{1,2},{2,1},{3,0},{4,7},{5,6},{6,5},{7,4},{8,11},{9,10},{10,... | collective-permute-start | bytes 1622024 | tf_op jit(solution)/shard_map/ppermute | solution.py:478
  43.5 14.8 %collective-permute-start.8 = (bf16[96,2560]{1,0:T(8,128)(2,1)}, bf16[96,2560]{1,0:T(8,128)(2,1)}, u32[]{:S(2)}, u32[]{:S(2)}) collective-permute-start(bf16[96,2560]{1,0:T(8,128)(2,1)} %collective-permute-done.2.refs_4_), channel_id=1, source_target_pairs={{0,8},{4,12},{8,16},{12,20},{16,24},{20,28},{24,0},{28,4},{1,9},{5... | collective-permute-start | bytes 1474568 | tf_op jit(solution)/shard_map/ppermute | solution.py:430
  45.2 13.9 %collective-permute-start.5 = (bf16[96,2560]{1,0:T(8,128)(2,1)S(1)}, bf16[96,2560]{1,0:T(8,128)(2,1)}, u32[]{:S(2)}, u32[]{:S(2)}) collective-permute-start(bf16[96,2560]{1,0:T(8,128)(2,1)S(1)} %bitcast.21), channel_id=1, source_target_pairs={{0,4},{4,0},{8,12},{12,8},{16,20},{20,16},{24,28},{28,24},{1,5},{5... | collective-permute-start | bytes 1474568 | tf_op jit(solution)/shard_map/ppermute | solution.py:433
  45.2 13.9 %collective-permute-start.6 = (bf16[96,2560]{1,0:T(8,128)(2,1)}, bf16[96,2560]{1,0:T(8,128)(2,1)}, u32[]{:S(2)}, u32[]{:S(2)}) collective-permute-start(bf16[96,2560]{1,0:T(8,128)(2,1)} %collective-permute-done.1.refs_2_), channel_id=1, source_target_pairs={{0,4},{4,0},{8,12},{12,8},{16,20},{20,16},{24,28},{28,24},{1,5},{5... | collective-permute-start | bytes 1474568 | tf_op jit(solution)/shard_map/ppermute | solution.py:433
  46.6 12.6 %collective-permute-start.7 = (bf16[96,2560]{1,0:T(8,128)(2,1)}, bf16[96,2560]{1,0:T(8,128)(2,1)}, u32[]{:S(2)}, u32[]{:S(2)}) collective-permute-start(bf16[96,2560]{1,0:T(8,128)(2,1)} %collective-permute-done.2.refs_4_), channel_id=1, source_target_pairs={{0,4},{4,0},{8,12},{12,8},{16,20},{20,16},{24,28},{28,24},{1,5},{5... | collective-permute-start | bytes 1474568 | tf_op jit(solution)/shard_map/ppermute | solution.py:433
  58.4 2.2 %collective-permute-start.9 = (bf16[96,2560]{1,0:T(8,128)(2,1)}, bf16[96,2560]{1,0:T(8,128)(2,1)}, u32[]{:S(2)}, u32[]{:S(2)}) collective-permute-start(bf16[96,2560]{1,0:T(8,128)(2,1)} %collective-permute-done.8.refs_6_), channel_id=1, source_target_pairs={{0,4},{4,0},{8,12},{12,8},{16,20},{20,16},{24,28},{28,24},{1,5},{5... | collective-permute-start | bytes 1474568 | tf_op jit(solution)/shard_map/ppermute | solution.py:433
  64.9 21.8 %collective-permute-start.10 = (bf16[256,1536]{1,0:T(8,128)(2,1)}, bf16[256,1536]{1,0:T(8,128)(2,1)}, u32[]{:S(2)}, u32[]{:S(2)}) collective-permute-start(bf16[256,1536]{1,0:T(8,128)(2,1)} %get-tuple-element.48.refs_0_), channel_id=1, source_target_pairs={{0,8},{4,12},{8,16},{12,20},{16,24},{20,28},{24,0},{28,4},{1,9},{5... | collective-permute-start | bytes 2359304 | tf_op jit(solution)/shard_map/ppermute | solution.py:430
  86.7 20.8 %collective-permute-start.11 = (bf16[256,1536]{1,0:T(8,128)(2,1)}, bf16[256,1536]{1,0:T(8,128)(2,1)S(1)}, u32[]{:S(2)}, u32[]{:S(2)}) collective-permute-start(bf16[256,1536]{1,0:T(8,128)(2,1)} %collective-permute-done.10.refs_2_), channel_id=1, source_target_pairs={{0,8},{4,12},{8,16},{12,20},{16,24},{20,28},{24,0},{28,4},{1,9},{5... | collective-permute-start | bytes 2359304 | tf_op jit(solution)/shard_map/ppermute | solution.py:430
  88.5 22.5 %all-to-all-start.1 = ((bf16[4,8,64,384]{3,2,1,0:T(8,128)(2,1)}), bf16[4,8,64,384]{3,2,1,0:T(8,128)(2,1)S(1)}, u32[]{:S(2)}, u32[]{:S(2)}) async-start(bf16[4,8,64,384]{3,2,1,0:T(8,128)(2,1)} %compact.1), calls=%async_computation.1 | async-start | bytes 3145728 | tf_op jit(solution)/shard_map/all_to_all | solution.py:436
  92.2 20.0 %collective-permute-start.14 = (bf16[256,1536]{1,0:T(8,128)(2,1)}, bf16[256,1536]{1,0:T(8,128)(2,1)}, u32[]{:S(2)}, u32[]{:S(2)}) collective-permute-start(bf16[256,1536]{1,0:T(8,128)(2,1)} %get-tuple-element.48.refs_0_), channel_id=1, source_target_pairs={{0,4},{4,0},{8,12},{12,8},{16,20},{20,16},{24,28},{28,24},{1,5},{5... | collective-permute-start | bytes 2359304 | tf_op jit(solution)/shard_map/ppermute | solution.py:433
  92.2 20.0 %collective-permute-start.15 = (bf16[256,1536]{1,0:T(8,128)(2,1)}, bf16[256,1536]{1,0:T(8,128)(2,1)}, u32[]{:S(2)}, u32[]{:S(2)}) collective-permute-start(bf16[256,1536]{1,0:T(8,128)(2,1)} %collective-permute-done.10.refs_2_), channel_id=1, source_target_pairs={{0,4},{4,0},{8,12},{12,8},{16,20},{20,16},{24,28},{28,24},{1,5},{5... | collective-permute-start | bytes 2359304 | tf_op jit(solution)/shard_map/ppermute | solution.py:433
  107.4 7.9 %collective-permute-start.13 = (bf16[256,1536]{1,0:T(8,128)(2,1)S(1)}, bf16[256,1536]{1,0:T(8,128)(2,1)}, u32[]{:S(2)}, u32[]{:S(2)}) collective-permute-start(bf16[256,1536]{1,0:T(8,128)(2,1)S(1)} %collective-permute-done.11.refs_0_), channel_id=1, source_target_pairs={{0,4},{4,0},{8,12},{12,8},{16,20},{20,16},{24,28},{28,24},{1,5},{5... | collective-permute-start | bytes 2359304 | tf_op jit(solution)/shard_map/ppermute | solution.py:433
  107.4 22.0 %collective-permute-start.12 = (bf16[256,1536]{1,0:T(8,128)(2,1)S(1)}, bf16[256,1536]{1,0:T(8,128)(2,1)S(1)}, u32[]{:S(2)}, u32[]{:S(2)}) collective-permute-start(bf16[256,1536]{1,0:T(8,128)(2,1)S(1)} %collective-permute-done.11.refs_0_), channel_id=1, source_target_pairs={{0,8},{4,12},{8,16},{12,20},{16,24},{20,28},{24,0},{28,4},{1,9},{5... | collective-permute-start | bytes 2359304 | tf_op jit(solution)/shard_map/ppermute | solution.py:430
  109.0 8.4 %collective-permute-start.16 = (f32[3,120,128]{2,1,0:T(8,128)}, f32[3,120,128]{2,1,0:T(8,128)S(1)}, u32[]{:S(2)}, u32[]{:S(2)}) collective-permute-start(f32[3,120,128]{2,1,0:T(8,128)} %heads.1), channel_id=1, source_target_pairs={{4,0},{8,4},{12,8},{16,12},{20,16},{24,20},{28,24},{5,1},{9,5},{13... | collective-permute-start | bytes 552968 | tf_op jit(solution)/shard_map/ppermute | solution.py:531
  115.3 17.7 %copy-start = (f32[1,1,506880]{2,1,0:T(1,128)S(1)}, f32[1,1,506880]{2,1,0:T(1,128)}, u32[]{:S(2)}) copy-start(f32[1,1,506880]{2,1,0:T(1,128)} %param.16) | copy-start | bytes 6082564
  115.3 17.7 %copy-start.1 = (f32[1,1,506880]{2,1,0:T(1,128)S(1)}, f32[1,1,506880]{2,1,0:T(1,128)}, u32[]{:S(2)}) copy-start(f32[1,1,506880]{2,1,0:T(1,128)} %param.17) | copy-start | bytes 6082564
  129.4 3.6 %collective-permute-start.17 = (bf16[256,1536]{1,0:T(8,128)(2,1)S(1)}, bf16[256,1536]{1,0:T(8,128)(2,1)S(1)}, u32[]{:S(2)}, u32[]{:S(2)}) collective-permute-start(bf16[256,1536]{1,0:T(8,128)(2,1)S(1)} %collective-permute-done.12.own_ref), channel_id=1, source_target_pairs={{0,4},{4,0},{8,12},{12,8},{16,20},{20,16},{24,28},{28,24},{1,5},{5... | collective-permute-start | bytes 2359304 | tf_op jit(solution)/shard_map/ppermute | solution.py:433
  (5 other events, 39.6 us)

commit v3 on v2

--- a/solution.py
+++ b/solution.py
@@ -484,7 +484,7 @@
             arrival = onward(held[-1])
             held.append(arrival)
             if k == chips - 2:
-                held[-1], arrived[1], arrived[2] = tied(held[-1], arrived[1], arrived[2])
+                held[-1], arrived[1] = tied(held[-1], arrived[1])
                 arrived[-1], windows, block = tied(arrived[-1], windows, held[-1])
                 other.append(swapped(block))
                 continue

time: 139 us -> 139 us (level)
  starting transfers between devices: 22.4 us -> 24.6 us
  waiting for transfers between devices: 87.5 us -> 85.3 us
    ppermute x3, waiting for transfers between devices: 22.2 us -> 11.2 us  [shards(): lax.ppermute(packed[k], 'expert', [(i, i ^ k) for i in range(experts)])]
    ppermute x6, waiting for transfers between devices: 60.6 us -> 71.1 us  [onward(): lax.ppermute(block, 'dp', [(i, (i + 2) % parts) for i in range(parts)])]
where the time goes in v3:
time: 139 us
  waiting for transfers between devices  85.3 us (61%)
  Pallas kernels  26.3 us (19%)
  starting transfers between devices  24.6 us (18%)
  local copies, waits for them, and re-layouts  1.78 us (1%)
    ppermute x6, waiting for transfers between devices, onward(): lax.ppermute(block, 'dp', [(i, (i + 2) % parts) for i in range(parts)])  71.1 us
    ppermute x3, waiting for transfers between devices, shards(): lax.ppermute(packed[k], 'expert', [(i, i ^ k) for i in range(experts)])  11.2 us
    pallas_call x7, Pallas kernels, call(): pl.pallas_call(kernel, out_shape=outs, in_specs=[smem()] * len(scalars) +...  9.95 us
    ppermute x6, starting transfers between devices, onward(): lax.ppermute(block, 'dp', [(i, (i + 2) % parts) for i in range(parts)])  8.31 us
    all_to_all x2, starting transfers between devices, exchanged(): return lax.all_to_all(block, axis, split_axis=0, concat_axis=0, tiled=True)  7.58 us
    pallas_call x1, Pallas kernels, shards(): pl.pallas_call(functools.partial(final_kernel, even_size=even_size, head_...  5.7 us
    pallas_call x1, Pallas kernels, shards(): pl.pallas_call(pack_kernel, out_shape=[struct((rows, token_count), f32),...  4.65 us
    ppermute x3, starting transfers between devices, shards(): lax.ppermute(packed[k], 'expert', [(i, i ^ k) for i in range(experts)])  4.5 us
  transfers between devices with their start and end apart: 20, of which 11 were waited for; matrix products, arithmetic and copies ran while one was open for 0% of the time, Pallas kernels for 12%

profile of v3, /device:TPU:0, one launch (start us, length us, event | category | flops | bytes accessed | tf_op | source)
XLA Modules:
  0.0 138.8 jit_solution(10023954090537774479)
XLA Ops:
  0.6 3.1 %collective-permute-start.1 = (bf16[96,2560]{1,0:T(8,128)(2,1)}, bf16[96,2560]{1,0:T(8,128)(2,1)S(1)}, u32[]{:S(2)}, u32[]{:S(2)}) collective-permute-start(bf16[96,2560]{1,0:T(8,128)(2,1)} %bitcast.20), channel_id=1, source_target_pairs={{0,8},{4,12},{8,16},{12,20},{16,24},{20,28},{24,0},{28,4},{1,9},{5... | collective-permute-start | bytes 1474568 | tf_op jit(solution)/shard_map/ppermute | solution.py:430
  3.7 4.6 %pack.1 = (f32[256,128]{1,0:T(8,128)}, f32[1,128]{1,0:T(1,128)}, bf16[64,4224]{1,0:T(8,128)(2,1)}, bf16[64,4224]{1,0:T(8,128)(2,1)}, bf16[64,4224]{1,0:T(8,128)(2,1)}, /*index=5*/bf16[64,4224]{1,0:T(8,128)(2,1)}) custom-call(s32[1]{0:T(128)} %bitcast.1.me_ref, s32[1,128]{1,0:T(1,128)} %bitcast.24, bf16[1,128]{1,0:T(2,128)(2,1)} %bitcast.25, ...), custom_call_target="tpu_custom_call" | custom-call | bytes 6000000 | tf_op jit(solution)/shard_map/pack/pallas_call | solution.py:443
  11.2 3.9 %all-to-all-start = ((bf16[8,128,384]{2,1,0:T(8,128)(2,1)}), bf16[8,128,384]{2,1,0:T(8,128)(2,1)S(1)}, u32[]{:S(2)}, u32[]{:S(2)}) async-start(bf16[8,128,384]{2,1,0:T(8,128)(2,1)} %window.1), calls=%async_computation | async-start | bytes 1572864 | tf_op jit(solution)/shard_map/all_to_all | solution.py:436
  15.1 1.5 %collective-permute-start.3 = (bf16[64,4224]{1,0:T(8,128)(2,1)}, bf16[64,4224]{1,0:T(8,128)(2,1)S(1)}, u32[]{:S(2)}, u32[]{:S(2)}) collective-permute-start(bf16[64,4224]{1,0:T(8,128)(2,1)} %get-tuple-element.33), channel_id=1, source_target_pairs={{0,1},{1,0},{2,3},{3,2},{4,5},{5,4},{6,7},{7,6},{8,9},{9,8},{10,11... | collective-permute-start | bytes 1622024 | tf_op jit(solution)/shard_map/ppermute | solution.py:478
  17.2 1.4 %collective-permute-start.2 = (bf16[96,2560]{1,0:T(8,128)(2,1)S(1)}, bf16[96,2560]{1,0:T(8,128)(2,1)}, u32[]{:S(2)}, u32[]{:S(2)}) collective-permute-start(bf16[96,2560]{1,0:T(8,128)(2,1)S(1)} %collective-permute-done.1.refs_2_), channel_id=1, source_target_pairs={{0,8},{4,12},{8,16},{12,20},{16,24},{20,28},{24,0},{28,4},{1,9},{5... | collective-permute-start | bytes 1474568 | tf_op jit(solution)/shard_map/ppermute | solution.py:430
  18.6 1.5 %collective-permute-start = (bf16[64,4224]{1,0:T(8,128)(2,1)}, bf16[64,4224]{1,0:T(8,128)(2,1)S(1)}, u32[]{:S(2)}, u32[]{:S(2)}) collective-permute-start(bf16[64,4224]{1,0:T(8,128)(2,1)} %get-tuple-element.31), channel_id=1, source_target_pairs={{0,3},{1,2},{2,1},{3,0},{4,7},{5,6},{6,5},{7,4},{8,11},{9,10},{10,... | collective-permute-start | bytes 1622024 | tf_op jit(solution)/shard_map/ppermute | solution.py:478
  20.1 10.3 %collective-permute-done.3.refs_1_ = bf16[64,4224]{1,0:T(8,128)(2,1)S(1)} collective-permute-done((bf16[64,4224]{1,0:T(8,128)(2,1)}, bf16[64,4224]{1,0:T(8,128)(2,1)S(1)}, u32[]{:S(2)}, u32[]{:S(2)}) %collective-permute-start.3) | collective-permute-done | bytes 540704 | tf_op jit(solution)/shard_map/ppermute | solution.py:478
  30.4 13.2 %collective-permute-done.2.refs_4_ = bf16[96,2560]{1,0:T(8,128)(2,1)} collective-permute-done((bf16[96,2560]{1,0:T(8,128)(2,1)S(1)}, bf16[96,2560]{1,0:T(8,128)(2,1)}, u32[]{:S(2)}, u32[]{:S(2)}) %collective-permute-start.2) | collective-permute-done | bytes 491552 | tf_op jit(solution)/shard_map/ppermute | solution.py:430
  43.5 1.6 %collective-permute-start.8 = (bf16[96,2560]{1,0:T(8,128)(2,1)}, bf16[96,2560]{1,0:T(8,128)(2,1)}, u32[]{:S(2)}, u32[]{:S(2)}) collective-permute-start(bf16[96,2560]{1,0:T(8,128)(2,1)} %collective-permute-done.2.refs_4_), channel_id=1, source_target_pairs={{0,8},{4,12},{8,16},{12,20},{16,24},{20,28},{24,0},{28,4},{1,9},{5... | collective-permute-start | bytes 1474568 | tf_op jit(solution)/shard_map/ppermute | solution.py:430
  45.1 1.5 %collective-permute-start.4 = (bf16[64,4224]{1,0:T(8,128)(2,1)}, bf16[64,4224]{1,0:T(8,128)(2,1)S(1)}, u32[]{:S(2)}, u32[]{:S(2)}) collective-permute-start(bf16[64,4224]{1,0:T(8,128)(2,1)} %get-tuple-element.38), channel_id=1, source_target_pairs={{0,2},{1,3},{2,0},{3,1},{4,6},{5,7},{6,4},{7,5},{8,10},{9,11},{10,... | collective-permute-start | bytes 1622024 | tf_op jit(solution)/shard_map/ppermute | solution.py:478
  47.2 11.1 %collective-permute-done.8.refs_6_ = bf16[96,2560]{1,0:T(8,128)(2,1)} collective-permute-done((bf16[96,2560]{1,0:T(8,128)(2,1)}, bf16[96,2560]{1,0:T(8,128)(2,1)}, u32[]{:S(2)}, u32[]{:S(2)}) %collective-permute-start.8) | collective-permute-done | bytes 491552 | tf_op jit(solution)/shard_map/ppermute | solution.py:430
  60.6 4.4 %rows.1 = (bf16[256,1536]{1,0:T(8,128)(2,1)}, f32[256,128]{1,0:T(8,128)S(1)}) custom-call(s32[1]{0:T(128)} %bitcast.position_ref, bf16[256,2560]{1,0:T(8,128)(2,1)S(1)} %get-tuple-element.40.grads_ref, f32[256,768]{1,0:T(8,128)S(1)} %get-tuple-element.41.gate_factor, f32[256,768]{1,0:T(8,128)S(1)} %get-tuple-element.42.up_factor, ...), custom_call_target="tpu_custom_call" | custom-call | flops 1006632960 | bytes 8000000 | tf_op jit(solution)/shard_map/rows/pallas_call | solution.py:504
  65.0 2.2 %collective-permute-start.10 = (bf16[256,1536]{1,0:T(8,128)(2,1)}, bf16[256,1536]{1,0:T(8,128)(2,1)}, u32[]{:S(2)}, u32[]{:S(2)}) collective-permute-start(bf16[256,1536]{1,0:T(8,128)(2,1)} %get-tuple-element.46.refs_0_), channel_id=1, source_target_pairs={{0,8},{4,12},{8,16},{12,20},{16,24},{20,28},{24,0},{28,4},{1,9},{5... | collective-permute-start | bytes 2359304 | tf_op jit(solution)/shard_map/ppermute | solution.py:430
  67.2 19.5 %collective-permute-done.10.refs_2_ = bf16[256,1536]{1,0:T(8,128)(2,1)} collective-permute-done((bf16[256,1536]{1,0:T(8,128)(2,1)}, bf16[256,1536]{1,0:T(8,128)(2,1)}, u32[]{:S(2)}, u32[]{:S(2)}) %collective-permute-start.10) | collective-permute-done | bytes 786464 | tf_op jit(solution)/shard_map/ppermute | solution.py:430
  86.7 1.8 %compact.1 = bf16[4,8,64,384]{3,2,1,0:T(8,128)(2,1)} custom-call(s32[1]{0:T(128)} %bitcast.position_ref, bf16[8,128,384]{2,1,0:T(8,128)(2,1)S(1)} %all-to-all-done.windows_ref, f32[256,128]{1,0:T(8,128)S(1)} %get-tuple-element.45.scores_ref), custom_call_target="tpu_custom_call" | custom-call | bytes 3000000 | tf_op jit(solution)/shard_map/compact/pallas_call | solution.py:378
  88.5 3.7 %all-to-all-start.1 = ((bf16[4,8,64,384]{3,2,1,0:T(8,128)(2,1)}), bf16[4,8,64,384]{3,2,1,0:T(8,128)(2,1)S(1)}, u32[]{:S(2)}, u32[]{:S(2)}) async-start(bf16[4,8,64,384]{3,2,1,0:T(8,128)(2,1)} %compact.1), calls=%async_computation.1 | async-start | bytes 3145728 | tf_op jit(solution)/shard_map/all_to_all | solution.py:436
  92.8 14.7 %collective-permute-done.11.refs_0_ = bf16[256,1536]{1,0:T(8,128)(2,1)S(1)} collective-permute-done((bf16[256,1536]{1,0:T(8,128)(2,1)}, bf16[256,1536]{1,0:T(8,128)(2,1)S(1)}, u32[]{:S(2)}, u32[]{:S(2)}) %collective-permute-start.11) | collective-permute-done | bytes 786464 | tf_op jit(solution)/shard_map/ppermute | solution.py:430
  107.5 1.6 %heads.1 = f32[3,120,128]{2,1,0:T(8,128)} custom-call(f32[3960,128]{1,0:T(8,128)} %bitcast.14, f32[3960,128]{1,0:T(8,128)} %bitcast.16, f32[3960,128]{1,0:T(8,128)} %bitcast.18), custom_call_target="tpu_custom_call" | custom-call | bytes 400000 | tf_op jit(solution)/shard_map/heads/pallas_call | solution.py:521
  112.3 3.1 %early1.1.refs_2_ = f32[336,1536]{1,0:T(8,128)S(1)} custom-call(s32[1]{0:T(128)} %bitcast.position_ref, bf16[8,336,256]{2,1,0:T(8,128)(2,1)S(1)} %turn.1.turned_ref, bf16[256,1536]{1,0:T(8,128)(2,1)} %get-tuple-element.46.refs_0_, bf16[256,1536]{1,0:T(8,128)(2,1)} %collective-permute-done.14.refs_1_, bf16[256,1536]{1,0:T(8,128)(2,1)} %collective-permute-done.10.refs_2_, ...), custom_call_target="tpu_custom_call" | custom-call | flops 1056964608 | bytes 8000000 | tf_op jit(solution)/shard_map/early1/pallas_call | solution.py:378
  115.4 2.0 %early2.1.early_ref = f32[336,1536]{1,0:T(8,128)S(1)} custom-call(s32[1]{0:T(128)} %bitcast.position_ref, bf16[8,336,256]{2,1,0:T(8,128)(2,1)S(1)} %turn.1.turned_ref, bf16[256,1536]{1,0:T(8,128)(2,1)S(1)} %collective-permute-done.11.refs_0_, bf16[256,1536]{1,0:T(8,128)(2,1)} %collective-permute-done.13.refs_1_, f32[336,1536]{1,0:T(8,128)S(1)} %early1.1.refs_2_), custom_call_target="tpu_custom_call" | custom-call | flops 528482304 | bytes 8000000 | tf_op jit(solution)/shard_map/early2/pallas_call | solution.py:378
  117.5 12.0 %collective-permute-done.12.own_ref = bf16[256,1536]{1,0:T(8,128)(2,1)S(1)} collective-permute-done((bf16[256,1536]{1,0:T(8,128)(2,1)S(1)}, bf16[256,1536]{1,0:T(8,128)(2,1)S(1)}, u32[]{:S(2)}, u32[]{:S(2)}) %collective-permute-start.12) | collective-permute-done | bytes 786464 | tf_op jit(solution)/shard_map/ppermute | solution.py:430
  129.4 1.7 %collective-permute-start.17 = (bf16[256,1536]{1,0:T(8,128)(2,1)S(1)}, bf16[256,1536]{1,0:T(8,128)(2,1)S(1)}, u32[]{:S(2)}, u32[]{:S(2)}) collective-permute-start(bf16[256,1536]{1,0:T(8,128)(2,1)S(1)} %collective-permute-done.12.own_ref), channel_id=1, source_target_pairs={{0,4},{4,0},{8,12},{12,8},{16,20},{20,16},{24,28},{28,24},{1,5},{5... | collective-permute-start | bytes 2359304 | tf_op jit(solution)/shard_map/ppermute | solution.py:433
  131.1 1.9 %collective-permute-done.17.other_ref = bf16[256,1536]{1,0:T(8,128)(2,1)S(1)} collective-permute-done((bf16[256,1536]{1,0:T(8,128)(2,1)S(1)}, bf16[256,1536]{1,0:T(8,128)(2,1)S(1)}, u32[]{:S(2)}, u32[]{:S(2)}) %collective-permute-start.17) | collective-permute-done | bytes 786464 | tf_op jit(solution)/shard_map/ppermute | solution.py:433
  133.1 5.7 %final.1 = (f32[3960,128]{1,0:T(8,128)}, f32[3960,128]{1,0:T(8,128)}, f32[3960,128]{1,0:T(8,128)}, bf16[320,1536]{1,0:T(8,128)(2,1)}) custom-call(s32[1]{0:T(128)} %bitcast.position_ref, s32[9]{0:T(128)S(1)} %copy-done.9, bf16[8,336,256]{2,1,0:T(8,128)(2,1)S(1)} %turn.1.turned_ref, f32[336,1536]{1,0:T(8,128)S(1)} %early2.1.early_ref, ...), custom_call_target="tpu_custom_call" | custom-call | flops 528482304 | bytes 25000000 | tf_op jit(solution)/shard_map/final/pallas_call | solution.py:590
  (49 shorter events, 9.9 us)
Async XLA Ops:
  0.6 16.5 %collective-permute-start.1 = (bf16[96,2560]{1,0:T(8,128)(2,1)}, bf16[96,2560]{1,0:T(8,128)(2,1)S(1)}, u32[]{:S(2)}, u32[]{:S(2)}) collective-permute-start(bf16[96,2560]{1,0:T(8,128)(2,1)} %bitcast.20), channel_id=1, source_target_pairs={{0,8},{4,12},{8,16},{12,20},{16,24},{20,28},{24,0},{28,4},{1,9},{5... | collective-permute-start | bytes 1474568 | tf_op jit(solution)/shard_map/ppermute | solution.py:430
  3.7 42.9 %copy-start.5 = (bf16[1,96,2560]{2,1,0:T(8,128)(2,1)S(1)}, bf16[1,96,2560]{2,1,0:T(8,128)(2,1)}, u32[]{:S(2)}) copy-start(bf16[1,96,2560]{2,1,0:T(8,128)(2,1)} %param.15) | copy-start | bytes 1474564
  10.1 49.2 %copy-start.4 = (bf16[64,4224]{1,0:T(8,128)(2,1)S(1)}, bf16[64,4224]{1,0:T(8,128)(2,1)}, u32[]{:S(2)}) copy-start(bf16[64,4224]{1,0:T(8,128)(2,1)} %get-tuple-element.36.refs_0_) | copy-start | bytes 1622020
  11.2 35.9 %all-to-all-start = ((bf16[8,128,384]{2,1,0:T(8,128)(2,1)}), bf16[8,128,384]{2,1,0:T(8,128)(2,1)S(1)}, u32[]{:S(2)}, u32[]{:S(2)}) async-start(bf16[8,128,384]{2,1,0:T(8,128)(2,1)} %window.1), calls=%async_computation | async-start | bytes 1572864 | tf_op jit(solution)/shard_map/all_to_all | solution.py:436
  15.1 15.3 %collective-permute-start.3 = (bf16[64,4224]{1,0:T(8,128)(2,1)}, bf16[64,4224]{1,0:T(8,128)(2,1)S(1)}, u32[]{:S(2)}, u32[]{:S(2)}) collective-permute-start(bf16[64,4224]{1,0:T(8,128)(2,1)} %get-tuple-element.33), channel_id=1, source_target_pairs={{0,1},{1,0},{2,3},{3,2},{4,5},{5,4},{6,7},{7,6},{8,9},{9,8},{10,11... | collective-permute-start | bytes 1622024 | tf_op jit(solution)/shard_map/ppermute | solution.py:478
  17.2 27.9 %copy-start.6 = (bf16[96,2560]{1,0:T(8,128)(2,1)}, bf16[96,2560]{1,0:T(8,128)(2,1)S(1)}, u32[]{:S(2)}) copy-start(bf16[96,2560]{1,0:T(8,128)(2,1)S(1)} %collective-permute-done.1.refs_2_) | copy-start | bytes 1474564
  17.2 26.4 %collective-permute-start.2 = (bf16[96,2560]{1,0:T(8,128)(2,1)S(1)}, bf16[96,2560]{1,0:T(8,128)(2,1)}, u32[]{:S(2)}, u32[]{:S(2)}) collective-permute-start(bf16[96,2560]{1,0:T(8,128)(2,1)S(1)} %collective-permute-done.1.refs_2_), channel_id=1, source_target_pairs={{0,8},{4,12},{8,16},{12,20},{16,24},{20,28},{24,0},{28,4},{1,9},{5... | collective-permute-start | bytes 1474568 | tf_op jit(solution)/shard_map/ppermute | solution.py:430
  18.6 28.5 %collective-permute-start = (bf16[64,4224]{1,0:T(8,128)(2,1)}, bf16[64,4224]{1,0:T(8,128)(2,1)S(1)}, u32[]{:S(2)}, u32[]{:S(2)}) collective-permute-start(bf16[64,4224]{1,0:T(8,128)(2,1)} %get-tuple-element.31), channel_id=1, source_target_pairs={{0,3},{1,2},{2,1},{3,0},{4,7},{5,6},{6,5},{7,4},{8,11},{9,10},{10,... | collective-permute-start | bytes 1622024 | tf_op jit(solution)/shard_map/ppermute | solution.py:478
  43.5 14.8 %collective-permute-start.8 = (bf16[96,2560]{1,0:T(8,128)(2,1)}, bf16[96,2560]{1,0:T(8,128)(2,1)}, u32[]{:S(2)}, u32[]{:S(2)}) collective-permute-start(bf16[96,2560]{1,0:T(8,128)(2,1)} %collective-permute-done.2.refs_4_), channel_id=1, source_target_pairs={{0,8},{4,12},{8,16},{12,20},{16,24},{20,28},{24,0},{28,4},{1,9},{5... | collective-permute-start | bytes 1474568 | tf_op jit(solution)/shard_map/ppermute | solution.py:430
  45.1 14.2 %collective-permute-start.4 = (bf16[64,4224]{1,0:T(8,128)(2,1)}, bf16[64,4224]{1,0:T(8,128)(2,1)S(1)}, u32[]{:S(2)}, u32[]{:S(2)}) collective-permute-start(bf16[64,4224]{1,0:T(8,128)(2,1)} %get-tuple-element.38), channel_id=1, source_target_pairs={{0,2},{1,3},{2,0},{3,1},{4,6},{5,7},{6,4},{7,5},{8,10},{9,11},{10,... | collective-permute-start | bytes 1622024 | tf_op jit(solution)/shard_map/ppermute | solution.py:478
  46.6 13.4 %collective-permute-start.5 = (bf16[96,2560]{1,0:T(8,128)(2,1)S(1)}, bf16[96,2560]{1,0:T(8,128)(2,1)}, u32[]{:S(2)}, u32[]{:S(2)}) collective-permute-start(bf16[96,2560]{1,0:T(8,128)(2,1)S(1)} %bitcast.21), channel_id=1, source_target_pairs={{0,4},{4,0},{8,12},{12,8},{16,20},{20,16},{24,28},{28,24},{1,5},{5... | collective-permute-start | bytes 1474568 | tf_op jit(solution)/shard_map/ppermute | solution.py:433
  46.6 13.4 %collective-permute-start.6 = (bf16[96,2560]{1,0:T(8,128)(2,1)}, bf16[96,2560]{1,0:T(8,128)(2,1)}, u32[]{:S(2)}, u32[]{:S(2)}) collective-permute-start(bf16[96,2560]{1,0:T(8,128)(2,1)} %copy-done.6), channel_id=1, source_target_pairs={{0,4},{4,0},{8,12},{12,8},{16,20},{20,16},{24,28},{28,24},{1,5},{5... | collective-permute-start | bytes 1474568 | tf_op jit(solution)/shard_map/ppermute | solution.py:433
  47.1 12.9 %collective-permute-start.7 = (bf16[96,2560]{1,0:T(8,128)(2,1)}, bf16[96,2560]{1,0:T(8,128)(2,1)}, u32[]{:S(2)}, u32[]{:S(2)}) collective-permute-start(bf16[96,2560]{1,0:T(8,128)(2,1)} %collective-permute-done.2.refs_4_), channel_id=1, source_target_pairs={{0,4},{4,0},{8,12},{12,8},{16,20},{20,16},{24,28},{28,24},{1,5},{5... | collective-permute-start | bytes 1474568 | tf_op jit(solution)/shard_map/ppermute | solution.py:433
  58.3 2.2 %collective-permute-start.9 = (bf16[96,2560]{1,0:T(8,128)(2,1)}, bf16[96,2560]{1,0:T(8,128)(2,1)}, u32[]{:S(2)}, u32[]{:S(2)}) collective-permute-start(bf16[96,2560]{1,0:T(8,128)(2,1)} %collective-permute-done.8.refs_6_), channel_id=1, source_target_pairs={{0,4},{4,0},{8,12},{12,8},{16,20},{20,16},{24,28},{28,24},{1,5},{5... | collective-permute-start | bytes 1474568 | tf_op jit(solution)/shard_map/ppermute | solution.py:433
  65.0 21.7 %collective-permute-start.10 = (bf16[256,1536]{1,0:T(8,128)(2,1)}, bf16[256,1536]{1,0:T(8,128)(2,1)}, u32[]{:S(2)}, u32[]{:S(2)}) collective-permute-start(bf16[256,1536]{1,0:T(8,128)(2,1)} %get-tuple-element.46.refs_0_), channel_id=1, source_target_pairs={{0,8},{4,12},{8,16},{12,20},{16,24},{20,28},{24,0},{28,4},{1,9},{5... | collective-permute-start | bytes 2359304 | tf_op jit(solution)/shard_map/ppermute | solution.py:430
  86.7 20.8 %collective-permute-start.11 = (bf16[256,1536]{1,0:T(8,128)(2,1)}, bf16[256,1536]{1,0:T(8,128)(2,1)S(1)}, u32[]{:S(2)}, u32[]{:S(2)}) collective-permute-start(bf16[256,1536]{1,0:T(8,128)(2,1)} %collective-permute-done.10.refs_2_), channel_id=1, source_target_pairs={{0,8},{4,12},{8,16},{12,20},{16,24},{20,28},{24,0},{28,4},{1,9},{5... | collective-permute-start | bytes 2359304 | tf_op jit(solution)/shard_map/ppermute | solution.py:430
  88.5 22.5 %all-to-all-start.1 = ((bf16[4,8,64,384]{3,2,1,0:T(8,128)(2,1)}), bf16[4,8,64,384]{3,2,1,0:T(8,128)(2,1)S(1)}, u32[]{:S(2)}, u32[]{:S(2)}) async-start(bf16[4,8,64,384]{3,2,1,0:T(8,128)(2,1)} %compact.1), calls=%async_computation.1 | async-start | bytes 3145728 | tf_op jit(solution)/shard_map/all_to_all | solution.py:436
  92.3 20.0 %collective-permute-start.14 = (bf16[256,1536]{1,0:T(8,128)(2,1)}, bf16[256,1536]{1,0:T(8,128)(2,1)}, u32[]{:S(2)}, u32[]{:S(2)}) collective-permute-start(bf16[256,1536]{1,0:T(8,128)(2,1)} %get-tuple-element.46.refs_0_), channel_id=1, source_target_pairs={{0,4},{4,0},{8,12},{12,8},{16,20},{20,16},{24,28},{28,24},{1,5},{5... | collective-permute-start | bytes 2359304 | tf_op jit(solution)/shard_map/ppermute | solution.py:433
  92.3 20.0 %collective-permute-start.15 = (bf16[256,1536]{1,0:T(8,128)(2,1)}, bf16[256,1536]{1,0:T(8,128)(2,1)}, u32[]{:S(2)}, u32[]{:S(2)}) collective-permute-start(bf16[256,1536]{1,0:T(8,128)(2,1)} %collective-permute-done.10.refs_2_), channel_id=1, source_target_pairs={{0,4},{4,0},{8,12},{12,8},{16,20},{20,16},{24,28},{28,24},{1,5},{5... | collective-permute-start | bytes 2359304 | tf_op jit(solution)/shard_map/ppermute | solution.py:433
  107.5 7.9 %collective-permute-start.13 = (bf16[256,1536]{1,0:T(8,128)(2,1)S(1)}, bf16[256,1536]{1,0:T(8,128)(2,1)}, u32[]{:S(2)}, u32[]{:S(2)}) collective-permute-start(bf16[256,1536]{1,0:T(8,128)(2,1)S(1)} %collective-permute-done.11.refs_0_), channel_id=1, source_target_pairs={{0,4},{4,0},{8,12},{12,8},{16,20},{20,16},{24,28},{28,24},{1,5},{5... | collective-permute-start | bytes 2359304 | tf_op jit(solution)/shard_map/ppermute | solution.py:433
  107.5 22.0 %collective-permute-start.12 = (bf16[256,1536]{1,0:T(8,128)(2,1)S(1)}, bf16[256,1536]{1,0:T(8,128)(2,1)S(1)}, u32[]{:S(2)}, u32[]{:S(2)}) collective-permute-start(bf16[256,1536]{1,0:T(8,128)(2,1)S(1)} %collective-permute-done.11.refs_0_), channel_id=1, source_target_pairs={{0,8},{4,12},{8,16},{12,20},{16,24},{20,28},{24,0},{28,4},{1,9},{5... | collective-permute-start | bytes 2359304 | tf_op jit(solution)/shard_map/ppermute | solution.py:430
  109.1 8.4 %collective-permute-start.16 = (f32[3,120,128]{2,1,0:T(8,128)}, f32[3,120,128]{2,1,0:T(8,128)S(1)}, u32[]{:S(2)}, u32[]{:S(2)}) collective-permute-start(f32[3,120,128]{2,1,0:T(8,128)} %heads.1), channel_id=1, source_target_pairs={{4,0},{8,4},{12,8},{16,12},{20,16},{24,20},{28,24},{5,1},{9,5},{13... | collective-permute-start | bytes 552968 | tf_op jit(solution)/shard_map/ppermute | solution.py:531
  115.4 17.7 %copy-start = (f32[1,1,506880]{2,1,0:T(1,128)S(1)}, f32[1,1,506880]{2,1,0:T(1,128)}, u32[]{:S(2)}) copy-start(f32[1,1,506880]{2,1,0:T(1,128)} %param.16) | copy-start | bytes 6082564
  129.4 3.6 %collective-permute-start.17 = (bf16[256,1536]{1,0:T(8,128)(2,1)S(1)}, bf16[256,1536]{1,0:T(8,128)(2,1)S(1)}, u32[]{:S(2)}, u32[]{:S(2)}) collective-permute-start(bf16[256,1536]{1,0:T(8,128)(2,1)S(1)} %collective-permute-done.12.own_ref), channel_id=1, source_target_pairs={{0,4},{4,0},{8,12},{12,8},{16,20},{20,16},{24,28},{28,24},{1,5},{5... | collective-permute-start | bytes 2359304 | tf_op jit(solution)/shard_map/ppermute | solution.py:433
  (7 other events, 59.5 us)

commit v4 on v2

--- a/solution.py
+++ b/solution.py
@@ -574,6 +574,8 @@
     arrival = joined
     for k in range(1, chips):
         arrival = onward(arrival) if k > 1 else step_one
+        if k == 2:
+            arrival, heads = tied(arrival, heads)
         if k > 2:
             pieces = steps.pop()
             if k == 3:
@@ -581,7 +583,7 @@
                 total = [begun]
             total = [early("early%d" % (k - 1), [k - 1], pieces, total)]
         if k == chips - 1:
-            arrival, total[0], router_grad, heads = tied(arrival, total[0], router_grad, heads)
+            arrival, total[0], router_grad = tied(arrival, total[0], router_grad)
         steps.append([arrival, swapped(arrival)])
     last = steps.pop()
     flat_rows = even_size // LANES

time: 139 us -> 139 us (level)
  starting transfers between devices: 22.4 us -> 23.9 us
  waiting for transfers between devices: 87.5 us -> 86 us
    ppermute x6, waiting for transfers between devices: 60.6 us -> 57.4 us  [onward(): lax.ppermute(block, 'dp', [(i, (i + 2) % parts) for i in range(parts)])]
  transfers between devices with their start and end apart: 20 -> 20, of which waited for: 11 -> 12; matrix products, arithmetic and copies ran while one was open for 0% -> 0% of each run, Pallas kernels for 12% -> 12%
where the time goes in v4:
time: 139 us
  waiting for transfers between devices  86 us (62%)
  Pallas kernels  26.3 us (19%)
  starting transfers between devices  23.9 us (17%)
  local copies, waits for them, and re-layouts  1.77 us (1%)
    ppermute x6, waiting for transfers between devices, onward(): lax.ppermute(block, 'dp', [(i, (i + 2) % parts) for i in range(parts)])  57.4 us
    ppermute x3, waiting for transfers between devices, shards(): lax.ppermute(packed[k], 'expert', [(i, i ^ k) for i in range(experts)])  22.2 us
    pallas_call x7, Pallas kernels, call(): pl.pallas_call(kernel, out_shape=outs, in_specs=[smem()] * len(scalars) +...  9.97 us
    ppermute x6, starting transfers between devices, onward(): lax.ppermute(block, 'dp', [(i, (i + 2) % parts) for i in range(parts)])  7.73 us
    all_to_all x2, starting transfers between devices, exchanged(): return lax.all_to_all(block, axis, split_axis=0, concat_axis=0, tiled=True)  7.58 us
    pallas_call x1, Pallas kernels, shards(): pl.pallas_call(functools.partial(final_kernel, even_size=even_size, head_...  5.72 us
    pallas_call x1, Pallas kernels, shards(): pl.pallas_call(pack_kernel, out_shape=[struct((rows, token_count), f32),...  4.66 us
    pallas_call x1, Pallas kernels, shards(): pl.pallas_call(functools.partial(row_kernel, chips=chips), out_shape=[str...  4.42 us
  transfers between devices with their start and end apart: 20, of which 12 were waited for; matrix products, arithmetic and copies ran while one was open for 0% of the time, Pallas kernels for 12%

profile of v4, /device:TPU:0, one launch (start us, length us, event | category | flops | bytes accessed | tf_op | source)
XLA Modules:
  0.0 138.9 jit_solution(1989726978395301891)
XLA Ops:
  0.6 3.1 %collective-permute-start.1 = (bf16[96,2560]{1,0:T(8,128)(2,1)}, bf16[96,2560]{1,0:T(8,128)(2,1)}, u32[]{:S(2)}, u32[]{:S(2)}) collective-permute-start(bf16[96,2560]{1,0:T(8,128)(2,1)} %bitcast.20), channel_id=1, source_target_pairs={{0,8},{4,12},{8,16},{12,20},{16,24},{20,28},{24,0},{28,4},{1,9},{5... | collective-permute-start | bytes 1474568 | tf_op jit(solution)/shard_map/ppermute | solution.py:430
  3.7 4.7 %pack.1 = (f32[256,128]{1,0:T(8,128)}, f32[1,128]{1,0:T(1,128)}, bf16[64,4224]{1,0:T(8,128)(2,1)}, bf16[64,4224]{1,0:T(8,128)(2,1)}, bf16[64,4224]{1,0:T(8,128)(2,1)}, /*index=5*/bf16[64,4224]{1,0:T(8,128)(2,1)}) custom-call(s32[1]{0:T(128)} %bitcast.1.me_ref, s32[1,128]{1,0:T(1,128)} %bitcast.24, bf16[1,128]{1,0:T(2,128)(2,1)} %bitcast.25, ...), custom_call_target="tpu_custom_call" | custom-call | bytes 6000000 | tf_op jit(solution)/shard_map/pack/pallas_call | solution.py:443
  11.2 3.9 %all-to-all-start = ((bf16[8,128,384]{2,1,0:T(8,128)(2,1)}), bf16[8,128,384]{2,1,0:T(8,128)(2,1)S(1)}, u32[]{:S(2)}, u32[]{:S(2)}) async-start(bf16[8,128,384]{2,1,0:T(8,128)(2,1)} %window.1), calls=%async_computation | async-start | bytes 1572864 | tf_op jit(solution)/shard_map/all_to_all | solution.py:436
  15.1 1.5 %collective-permute-start.3 = (bf16[64,4224]{1,0:T(8,128)(2,1)}, bf16[64,4224]{1,0:T(8,128)(2,1)S(1)}, u32[]{:S(2)}, u32[]{:S(2)}) collective-permute-start(bf16[64,4224]{1,0:T(8,128)(2,1)} %get-tuple-element.35), channel_id=1, source_target_pairs={{0,1},{1,0},{2,3},{3,2},{4,5},{5,4},{6,7},{7,6},{8,9},{9,8},{10,11... | collective-permute-start | bytes 1622024 | tf_op jit(solution)/shard_map/ppermute | solution.py:478
  16.6 1.5 %collective-permute-start.4 = (bf16[64,4224]{1,0:T(8,128)(2,1)}, bf16[64,4224]{1,0:T(8,128)(2,1)S(1)}, u32[]{:S(2)}, u32[]{:S(2)}) collective-permute-start(bf16[64,4224]{1,0:T(8,128)(2,1)} %get-tuple-element.36), channel_id=1, source_target_pairs={{0,2},{1,3},{2,0},{3,1},{4,6},{5,7},{6,4},{7,5},{8,10},{9,11},{10,... | collective-permute-start | bytes 1622024 | tf_op jit(solution)/shard_map/ppermute | solution.py:478
  18.1 2.0 %collective-permute-start.2 = (bf16[96,2560]{1,0:T(8,128)(2,1)}, bf16[96,2560]{1,0:T(8,128)(2,1)}, u32[]{:S(2)}, u32[]{:S(2)}) collective-permute-start(bf16[96,2560]{1,0:T(8,128)(2,1)} %collective-permute-done.1.refs_2_), channel_id=1, source_target_pairs={{0,8},{4,12},{8,16},{12,20},{16,24},{20,28},{24,0},{28,4},{1,9},{5... | collective-permute-start | bytes 1474568 | tf_op jit(solution)/shard_map/ppermute | solution.py:430
  20.6 9.8 %collective-permute-done.3.refs_1_ = bf16[64,4224]{1,0:T(8,128)(2,1)S(1)} collective-permute-done((bf16[64,4224]{1,0:T(8,128)(2,1)}, bf16[64,4224]{1,0:T(8,128)(2,1)S(1)}, u32[]{:S(2)}, u32[]{:S(2)}) %collective-permute-start.3) | collective-permute-done | bytes 540704 | tf_op jit(solution)/shard_map/ppermute | solution.py:478
  30.4 12.4 %collective-permute-done.4.refs_2_ = bf16[64,4224]{1,0:T(8,128)(2,1)S(1)} collective-permute-done((bf16[64,4224]{1,0:T(8,128)(2,1)}, bf16[64,4224]{1,0:T(8,128)(2,1)S(1)}, u32[]{:S(2)}, u32[]{:S(2)}) %collective-permute-start.4) | collective-permute-done | bytes 540704 | tf_op jit(solution)/shard_map/ppermute | solution.py:478
  43.5 1.7 %collective-permute-start.8 = (bf16[96,2560]{1,0:T(8,128)(2,1)}, bf16[96,2560]{1,0:T(8,128)(2,1)}, u32[]{:S(2)}, u32[]{:S(2)}) collective-permute-start(bf16[96,2560]{1,0:T(8,128)(2,1)} %collective-permute-done.2.refs_4_), channel_id=1, source_target_pairs={{0,8},{4,12},{8,16},{12,20},{16,24},{20,28},{24,0},{28,4},{1,9},{5... | collective-permute-start | bytes 1474568 | tf_op jit(solution)/shard_map/ppermute | solution.py:430
  46.6 11.7 %collective-permute-done.8.refs_6_ = bf16[96,2560]{1,0:T(8,128)(2,1)} collective-permute-done((bf16[96,2560]{1,0:T(8,128)(2,1)}, bf16[96,2560]{1,0:T(8,128)(2,1)}, u32[]{:S(2)}, u32[]{:S(2)}) %collective-permute-start.8) | collective-permute-done | bytes 491552 | tf_op jit(solution)/shard_map/ppermute | solution.py:430
  59.2 1.4 %collective-permute-done.9.refs_7_ = bf16[96,2560]{1,0:T(8,128)(2,1)} collective-permute-done((bf16[96,2560]{1,0:T(8,128)(2,1)}, bf16[96,2560]{1,0:T(8,128)(2,1)}, u32[]{:S(2)}, u32[]{:S(2)}) %collective-permute-start.9) | collective-permute-done | bytes 491552 | tf_op jit(solution)/shard_map/ppermute | solution.py:433
  60.6 4.4 %rows.1 = (bf16[256,1536]{1,0:T(8,128)(2,1)}, f32[256,128]{1,0:T(8,128)S(1)}) custom-call(s32[1]{0:T(128)} %bitcast.position_ref, bf16[256,2560]{1,0:T(8,128)(2,1)S(1)} %get-tuple-element.43.grads_ref, f32[256,768]{1,0:T(8,128)S(1)} %get-tuple-element.44.gate_factor, f32[256,768]{1,0:T(8,128)S(1)} %get-tuple-element.45.up_factor, ...), custom_call_target="tpu_custom_call" | custom-call | flops 1006632960 | bytes 8000000 | tf_op jit(solution)/shard_map/rows/pallas_call | solution.py:504
  65.4 21.3 %collective-permute-done.10.refs_2_ = bf16[256,1536]{1,0:T(8,128)(2,1)} collective-permute-done((bf16[256,1536]{1,0:T(8,128)(2,1)}, bf16[256,1536]{1,0:T(8,128)(2,1)}, u32[]{:S(2)}, u32[]{:S(2)}) %collective-permute-start.10) | collective-permute-done | bytes 786464 | tf_op jit(solution)/shard_map/ppermute | solution.py:430
  86.7 1.8 %compact.1 = bf16[4,8,64,384]{3,2,1,0:T(8,128)(2,1)} custom-call(s32[1]{0:T(128)} %bitcast.position_ref, bf16[8,128,384]{2,1,0:T(8,128)(2,1)S(1)} %all-to-all-done.windows_ref, f32[256,128]{1,0:T(8,128)S(1)} %get-tuple-element.48.scores_ref), custom_call_target="tpu_custom_call" | custom-call | bytes 3000000 | tf_op jit(solution)/shard_map/compact/pallas_call | solution.py:378
  88.5 3.7 %all-to-all-start.1 = ((bf16[4,8,64,384]{3,2,1,0:T(8,128)(2,1)}), bf16[4,8,64,384]{3,2,1,0:T(8,128)(2,1)S(1)}, u32[]{:S(2)}, u32[]{:S(2)}) async-start(bf16[4,8,64,384]{3,2,1,0:T(8,128)(2,1)} %compact.1), calls=%async_computation.1 | async-start | bytes 3145728 | tf_op jit(solution)/shard_map/all_to_all | solution.py:436
  92.3 1.6 %heads.1 = f32[3,120,128]{2,1,0:T(8,128)} custom-call(f32[3960,128]{1,0:T(8,128)} %bitcast.14, f32[3960,128]{1,0:T(8,128)} %bitcast.16, f32[3960,128]{1,0:T(8,128)} %bitcast.18), custom_call_target="tpu_custom_call" | custom-call | bytes 400000 | tf_op jit(solution)/shard_map/heads/pallas_call | solution.py:521
  93.8 1.4 %collective-permute-start.12 = (f32[3,120,128]{2,1,0:T(8,128)}, f32[3,120,128]{2,1,0:T(8,128)S(1)}, u32[]{:S(2)}, u32[]{:S(2)}) collective-permute-start(f32[3,120,128]{2,1,0:T(8,128)} %heads.1), channel_id=1, source_target_pairs={{4,0},{8,4},{12,8},{16,12},{20,16},{24,20},{28,24},{5,1},{9,5},{13... | collective-permute-start | bytes 552968 | tf_op jit(solution)/shard_map/ppermute | solution.py:531
  97.5 10.2 %collective-permute-done.11.refs_0_ = bf16[256,1536]{1,0:T(8,128)(2,1)S(1)} collective-permute-done((bf16[256,1536]{1,0:T(8,128)(2,1)}, bf16[256,1536]{1,0:T(8,128)(2,1)S(1)}, u32[]{:S(2)}, u32[]{:S(2)}) %collective-permute-start.11) | collective-permute-done | bytes 786464 | tf_op jit(solution)/shard_map/ppermute | solution.py:430
  107.7 1.9 %collective-permute-start.14 = (bf16[256,1536]{1,0:T(8,128)(2,1)S(1)}, bf16[256,1536]{1,0:T(8,128)(2,1)}, u32[]{:S(2)}, u32[]{:S(2)}) collective-permute-start(bf16[256,1536]{1,0:T(8,128)(2,1)S(1)} %collective-permute-done.11.refs_0_), channel_id=1, source_target_pairs={{0,4},{4,0},{8,12},{12,8},{16,20},{20,16},{24,28},{28,24},{1,5},{5... | collective-permute-start | bytes 2359304 | tf_op jit(solution)/shard_map/ppermute | solution.py:433
  112.3 3.1 %early1.1.refs_2_ = f32[336,1536]{1,0:T(8,128)S(1)} custom-call(s32[1]{0:T(128)} %bitcast.position_ref, bf16[8,336,256]{2,1,0:T(8,128)(2,1)S(1)} %turn.1.turned_ref, bf16[256,1536]{1,0:T(8,128)(2,1)} %get-tuple-element.49.refs_0_, bf16[256,1536]{1,0:T(8,128)(2,1)} %collective-permute-done.15.refs_1_, bf16[256,1536]{1,0:T(8,128)(2,1)} %collective-permute-done.10.refs_2_, ...), custom_call_target="tpu_custom_call" | custom-call | flops 1056964608 | bytes 8000000 | tf_op jit(solution)/shard_map/early1/pallas_call | solution.py:378
  115.4 2.0 %early2.1.early_ref = f32[336,1536]{1,0:T(8,128)S(1)} custom-call(s32[1]{0:T(128)} %bitcast.position_ref, bf16[8,336,256]{2,1,0:T(8,128)(2,1)S(1)} %turn.1.turned_ref, bf16[256,1536]{1,0:T(8,128)(2,1)S(1)} %collective-permute-done.11.refs_0_, bf16[256,1536]{1,0:T(8,128)(2,1)} %collective-permute-done.14.refs_1_, f32[336,1536]{1,0:T(8,128)S(1)} %early1.1.refs_2_), custom_call_target="tpu_custom_call" | custom-call | flops 528482304 | bytes 8000000 | tf_op jit(solution)/shard_map/early2/pallas_call | solution.py:378
  117.5 13.4 %collective-permute-done.13.own_ref = bf16[256,1536]{1,0:T(8,128)(2,1)S(1)} collective-permute-done((bf16[256,1536]{1,0:T(8,128)(2,1)S(1)}, bf16[256,1536]{1,0:T(8,128)(2,1)S(1)}, u32[]{:S(2)}, u32[]{:S(2)}) %collective-permute-start.13) | collective-permute-done | bytes 786464 | tf_op jit(solution)/shard_map/ppermute | solution.py:430
  130.8 2.3 %collective-permute-done.17.other_ref = bf16[256,1536]{1,0:T(8,128)(2,1)S(1)} collective-permute-done((bf16[256,1536]{1,0:T(8,128)(2,1)S(1)}, bf16[256,1536]{1,0:T(8,128)(2,1)S(1)}, u32[]{:S(2)}, u32[]{:S(2)}) %collective-permute-start.17) | collective-permute-done | bytes 786464 | tf_op jit(solution)/shard_map/ppermute | solution.py:433
  133.2 5.7 %final.1 = (f32[3960,128]{1,0:T(8,128)}, f32[3960,128]{1,0:T(8,128)}, f32[3960,128]{1,0:T(8,128)}, bf16[320,1536]{1,0:T(8,128)(2,1)}) custom-call(s32[1]{0:T(128)} %bitcast.position_ref, s32[9]{0:T(128)S(1)} %copy-done.7, bf16[8,336,256]{2,1,0:T(8,128)(2,1)S(1)} %turn.1.turned_ref, f32[336,1536]{1,0:T(8,128)S(1)} %early2.1.early_ref, ...), custom_call_target="tpu_custom_call" | custom-call | flops 528482304 | bytes 25000000 | tf_op jit(solution)/shard_map/final/pallas_call | solution.py:592
  (45 shorter events, 11.6 us)
Async XLA Ops:
  0.6 17.5 %collective-permute-start.1 = (bf16[96,2560]{1,0:T(8,128)(2,1)}, bf16[96,2560]{1,0:T(8,128)(2,1)}, u32[]{:S(2)}, u32[]{:S(2)}) collective-permute-start(bf16[96,2560]{1,0:T(8,128)(2,1)} %bitcast.20), channel_id=1, source_target_pairs={{0,8},{4,12},{8,16},{12,20},{16,24},{20,28},{24,0},{28,4},{1,9},{5... | collective-permute-start | bytes 1474568 | tf_op jit(solution)/shard_map/ppermute | solution.py:430
  3.7 41.5 %copy-start.5 = (bf16[1,96,2560]{2,1,0:T(8,128)(2,1)S(1)}, bf16[1,96,2560]{2,1,0:T(8,128)(2,1)}, u32[]{:S(2)}) copy-start(bf16[1,96,2560]{2,1,0:T(8,128)(2,1)} %param.15) | copy-start | bytes 1474564
  10.1 48.2 %copy-start.4 = (bf16[64,4224]{1,0:T(8,128)(2,1)S(1)}, bf16[64,4224]{1,0:T(8,128)(2,1)}, u32[]{:S(2)}) copy-start(bf16[64,4224]{1,0:T(8,128)(2,1)} %get-tuple-element.39.refs_0_) | copy-start | bytes 1622020
  11.2 35.4 %all-to-all-start = ((bf16[8,128,384]{2,1,0:T(8,128)(2,1)}), bf16[8,128,384]{2,1,0:T(8,128)(2,1)S(1)}, u32[]{:S(2)}, u32[]{:S(2)}) async-start(bf16[8,128,384]{2,1,0:T(8,128)(2,1)} %window.1), calls=%async_computation | async-start | bytes 1572864 | tf_op jit(solution)/shard_map/all_to_all | solution.py:436
  15.1 15.3 %collective-permute-start.3 = (bf16[64,4224]{1,0:T(8,128)(2,1)}, bf16[64,4224]{1,0:T(8,128)(2,1)S(1)}, u32[]{:S(2)}, u32[]{:S(2)}) collective-permute-start(bf16[64,4224]{1,0:T(8,128)(2,1)} %get-tuple-element.35), channel_id=1, source_target_pairs={{0,1},{1,0},{2,3},{3,2},{4,5},{5,4},{6,7},{7,6},{8,9},{9,8},{10,11... | collective-permute-start | bytes 1622024 | tf_op jit(solution)/shard_map/ppermute | solution.py:478
  16.6 26.2 %collective-permute-start.4 = (bf16[64,4224]{1,0:T(8,128)(2,1)}, bf16[64,4224]{1,0:T(8,128)(2,1)S(1)}, u32[]{:S(2)}, u32[]{:S(2)}) collective-permute-start(bf16[64,4224]{1,0:T(8,128)(2,1)} %get-tuple-element.36), channel_id=1, source_target_pairs={{0,2},{1,3},{2,0},{3,1},{4,6},{5,7},{6,4},{7,5},{8,10},{9,11},{10,... | collective-permute-start | bytes 1622024 | tf_op jit(solution)/shard_map/ppermute | solution.py:478
  18.1 25.4 %collective-permute-start.2 = (bf16[96,2560]{1,0:T(8,128)(2,1)}, bf16[96,2560]{1,0:T(8,128)(2,1)}, u32[]{:S(2)}, u32[]{:S(2)}) collective-permute-start(bf16[96,2560]{1,0:T(8,128)(2,1)} %collective-permute-done.1.refs_2_), channel_id=1, source_target_pairs={{0,8},{4,12},{8,16},{12,20},{16,24},{20,28},{24,0},{28,4},{1,9},{5... | collective-permute-start | bytes 1474568 | tf_op jit(solution)/shard_map/ppermute | solution.py:430
  20.1 25.6 %collective-permute-start = (bf16[64,4224]{1,0:T(8,128)(2,1)}, bf16[64,4224]{1,0:T(8,128)(2,1)S(1)}, u32[]{:S(2)}, u32[]{:S(2)}) collective-permute-start(bf16[64,4224]{1,0:T(8,128)(2,1)} %get-tuple-element.33), channel_id=1, source_target_pairs={{0,3},{1,2},{2,1},{3,0},{4,7},{5,6},{6,5},{7,4},{8,11},{9,10},{10,... | collective-permute-start | bytes 1622024 | tf_op jit(solution)/shard_map/ppermute | solution.py:478
  43.5 14.8 %collective-permute-start.8 = (bf16[96,2560]{1,0:T(8,128)(2,1)}, bf16[96,2560]{1,0:T(8,128)(2,1)}, u32[]{:S(2)}, u32[]{:S(2)}) collective-permute-start(bf16[96,2560]{1,0:T(8,128)(2,1)} %collective-permute-done.2.refs_4_), channel_id=1, source_target_pairs={{0,8},{4,12},{8,16},{12,20},{16,24},{20,28},{24,0},{28,4},{1,9},{5... | collective-permute-start | bytes 1474568 | tf_op jit(solution)/shard_map/ppermute | solution.py:430
  45.2 13.9 %collective-permute-start.5 = (bf16[96,2560]{1,0:T(8,128)(2,1)S(1)}, bf16[96,2560]{1,0:T(8,128)(2,1)}, u32[]{:S(2)}, u32[]{:S(2)}) collective-permute-start(bf16[96,2560]{1,0:T(8,128)(2,1)S(1)} %bitcast.21), channel_id=1, source_target_pairs={{0,4},{4,0},{8,12},{12,8},{16,20},{20,16},{24,28},{28,24},{1,5},{5... | collective-permute-start | bytes 1474568 | tf_op jit(solution)/shard_map/ppermute | solution.py:433
  45.2 13.9 %collective-permute-start.6 = (bf16[96,2560]{1,0:T(8,128)(2,1)}, bf16[96,2560]{1,0:T(8,128)(2,1)}, u32[]{:S(2)}, u32[]{:S(2)}) collective-permute-start(bf16[96,2560]{1,0:T(8,128)(2,1)} %collective-permute-done.1.refs_2_), channel_id=1, source_target_pairs={{0,4},{4,0},{8,12},{12,8},{16,20},{20,16},{24,28},{28,24},{1,5},{5... | collective-permute-start | bytes 1474568 | tf_op jit(solution)/shard_map/ppermute | solution.py:433
  46.6 12.6 %collective-permute-start.7 = (bf16[96,2560]{1,0:T(8,128)(2,1)}, bf16[96,2560]{1,0:T(8,128)(2,1)}, u32[]{:S(2)}, u32[]{:S(2)}) collective-permute-start(bf16[96,2560]{1,0:T(8,128)(2,1)} %collective-permute-done.2.refs_4_), channel_id=1, source_target_pairs={{0,4},{4,0},{8,12},{12,8},{16,20},{20,16},{24,28},{28,24},{1,5},{5... | collective-permute-start | bytes 1474568 | tf_op jit(solution)/shard_map/ppermute | solution.py:433
  58.4 2.2 %collective-permute-start.9 = (bf16[96,2560]{1,0:T(8,128)(2,1)}, bf16[96,2560]{1,0:T(8,128)(2,1)}, u32[]{:S(2)}, u32[]{:S(2)}) collective-permute-start(bf16[96,2560]{1,0:T(8,128)(2,1)} %collective-permute-done.8.refs_6_), channel_id=1, source_target_pairs={{0,4},{4,0},{8,12},{12,8},{16,20},{20,16},{24,28},{28,24},{1,5},{5... | collective-permute-start | bytes 1474568 | tf_op jit(solution)/shard_map/ppermute | solution.py:433
  65.0 21.7 %collective-permute-start.10 = (bf16[256,1536]{1,0:T(8,128)(2,1)}, bf16[256,1536]{1,0:T(8,128)(2,1)}, u32[]{:S(2)}, u32[]{:S(2)}) collective-permute-start(bf16[256,1536]{1,0:T(8,128)(2,1)} %get-tuple-element.49.refs_0_), channel_id=1, source_target_pairs={{0,8},{4,12},{8,16},{12,20},{16,24},{20,28},{24,0},{28,4},{1,9},{5... | collective-permute-start | bytes 2359304 | tf_op jit(solution)/shard_map/ppermute | solution.py:430
  86.7 20.9 %collective-permute-start.11 = (bf16[256,1536]{1,0:T(8,128)(2,1)}, bf16[256,1536]{1,0:T(8,128)(2,1)S(1)}, u32[]{:S(2)}, u32[]{:S(2)}) collective-permute-start(bf16[256,1536]{1,0:T(8,128)(2,1)} %collective-permute-done.10.refs_2_), channel_id=1, source_target_pairs={{0,8},{4,12},{8,16},{12,20},{16,24},{20,28},{24,0},{28,4},{1,9},{5... | collective-permute-start | bytes 2359304 | tf_op jit(solution)/shard_map/ppermute | solution.py:430
  88.5 22.5 %all-to-all-start.1 = ((bf16[4,8,64,384]{3,2,1,0:T(8,128)(2,1)}), bf16[4,8,64,384]{3,2,1,0:T(8,128)(2,1)S(1)}, u32[]{:S(2)}, u32[]{:S(2)}) async-start(bf16[4,8,64,384]{3,2,1,0:T(8,128)(2,1)} %compact.1), calls=%async_computation.1 | async-start | bytes 3145728 | tf_op jit(solution)/shard_map/all_to_all | solution.py:436
  93.8 3.6 %collective-permute-start.12 = (f32[3,120,128]{2,1,0:T(8,128)}, f32[3,120,128]{2,1,0:T(8,128)S(1)}, u32[]{:S(2)}, u32[]{:S(2)}) collective-permute-start(f32[3,120,128]{2,1,0:T(8,128)} %heads.1), channel_id=1, source_target_pairs={{4,0},{8,4},{12,8},{16,12},{20,16},{24,20},{28,24},{5,1},{9,5},{13... | collective-permute-start | bytes 552968 | tf_op jit(solution)/shard_map/ppermute | solution.py:531
  95.3 17.0 %collective-permute-start.15 = (bf16[256,1536]{1,0:T(8,128)(2,1)}, bf16[256,1536]{1,0:T(8,128)(2,1)}, u32[]{:S(2)}, u32[]{:S(2)}) collective-permute-start(bf16[256,1536]{1,0:T(8,128)(2,1)} %get-tuple-element.49.refs_0_), channel_id=1, source_target_pairs={{0,4},{4,0},{8,12},{12,8},{16,20},{20,16},{24,28},{28,24},{1,5},{5... | collective-permute-start | bytes 2359304 | tf_op jit(solution)/shard_map/ppermute | solution.py:433
  96.5 15.8 %collective-permute-start.16 = (bf16[256,1536]{1,0:T(8,128)(2,1)}, bf16[256,1536]{1,0:T(8,128)(2,1)}, u32[]{:S(2)}, u32[]{:S(2)}) collective-permute-start(bf16[256,1536]{1,0:T(8,128)(2,1)} %collective-permute-done.10.refs_2_), channel_id=1, source_target_pairs={{0,4},{4,0},{8,12},{12,8},{16,20},{20,16},{24,28},{28,24},{1,5},{5... | collective-permute-start | bytes 2359304 | tf_op jit(solution)/shard_map/ppermute | solution.py:433
  107.7 7.8 %collective-permute-start.14 = (bf16[256,1536]{1,0:T(8,128)(2,1)S(1)}, bf16[256,1536]{1,0:T(8,128)(2,1)}, u32[]{:S(2)}, u32[]{:S(2)}) collective-permute-start(bf16[256,1536]{1,0:T(8,128)(2,1)S(1)} %collective-permute-done.11.refs_0_), channel_id=1, source_target_pairs={{0,4},{4,0},{8,12},{12,8},{16,20},{20,16},{24,28},{28,24},{1,5},{5... | collective-permute-start | bytes 2359304 | tf_op jit(solution)/shard_map/ppermute | solution.py:433
  109.6 21.2 %collective-permute-start.13 = (bf16[256,1536]{1,0:T(8,128)(2,1)S(1)}, bf16[256,1536]{1,0:T(8,128)(2,1)S(1)}, u32[]{:S(2)}, u32[]{:S(2)}) collective-permute-start(bf16[256,1536]{1,0:T(8,128)(2,1)S(1)} %collective-permute-done.11.refs_0_), channel_id=1, source_target_pairs={{0,8},{4,12},{8,16},{12,20},{16,24},{20,28},{24,0},{28,4},{1,9},{5... | collective-permute-start | bytes 2359304 | tf_op jit(solution)/shard_map/ppermute | solution.py:430
  115.4 17.8 %copy-start = (f32[1,1,506880]{2,1,0:T(1,128)S(1)}, f32[1,1,506880]{2,1,0:T(1,128)}, u32[]{:S(2)}) copy-start(f32[1,1,506880]{2,1,0:T(1,128)} %param.16) | copy-start | bytes 6082564
  115.4 17.8 %copy-start.1 = (f32[1,1,506880]{2,1,0:T(1,128)S(1)}, f32[1,1,506880]{2,1,0:T(1,128)}, u32[]{:S(2)}) copy-start(f32[1,1,506880]{2,1,0:T(1,128)} %param.17) | copy-start | bytes 6082564
  130.8 2.3 %collective-permute-start.17 = (bf16[256,1536]{1,0:T(8,128)(2,1)S(1)}, bf16[256,1536]{1,0:T(8,128)(2,1)S(1)}, u32[]{:S(2)}, u32[]{:S(2)}) collective-permute-start(bf16[256,1536]{1,0:T(8,128)(2,1)S(1)} %collective-permute-done.13.own_ref), channel_id=1, source_target_pairs={{0,4},{4,0},{8,12},{12,8},{16,20},{20,16},{24,28},{28,24},{1,5},{5... | collective-permute-start | bytes 2359304 | tf_op jit(solution)/shard_map/ppermute | solution.py:433
  (5 other events, 54.9 us)
